TPU v7x, 32 devices: a whole 2x2x4 slice. The times are simulated.
32 devices in a mesh: batch: 16 (over z, y, x), mp: 2 (over core).
Axes of the slice: x: 2, y: 2, z: 4, core: 2. Of those that a mesh axis runs over, the one named last changes fastest.
Arguments:
- hidden_in: bfloat16 [32, 1024, 768], P('batch', 'mp'), may hold values from -6 to 6
- memory_flags: int32 [32], P('batch'), may hold values 0 or 1
- memory_coeffs: bfloat16 [32, 256, 768], P('batch', 'mp'), may hold values from -6 to 6
- first_gain: float32 [768], replicated, may hold values from 0.25 to 1.75
- first_bias: float32 [768], replicated, may hold values from -1.5 to 1.5
- query_key_value_matrix: bfloat16 [768, 3, 768], P(None, None, 'mp'), may hold values from -0.21875 to 0.21875
- qv_bias: bfloat16 [2, 768], P(None, 'mp'), may hold values from -1.5 to 1.5
- memory_weight: bfloat16 [2, 12, 256], P(None, 'mp'), may hold values from -0.1875 to 0.1875
- memory_bias: bfloat16 [2, 12], P(None, 'mp'), may hold values from -1.5 to 1.5
- output_matrix: bfloat16 [768, 768], P('mp'), may hold values from -1.25 to 1.25
- out_bias: float32 [768], replicated, may hold values from -1.5 to 1.5
- second_gain: float32 [768], replicated, may hold values from 0.25 to 1.75
- second_bias: float32 [768], replicated, may hold values from -1.5 to 1.5
- up_matrix: bfloat16 [768, 3072], P(None, 'mp'), may hold values from -0.21875 to 0.21875
- up_bias_vector: bfloat16 [3072], P('mp'), may hold values from -1.5 to 1.5
- down_matrix: bfloat16 [3072, 768], P('mp'), may hold values from -0.109375 to 0.109375
- down_bias: float32 [768], replicated, may hold values from -1.5 to 1.5
- out_grad: bfloat16 [32, 1024, 768], P('batch', 'mp'), may hold values from -6 to 6
Outputs:
- block_out: bfloat16 [32, 1024, 768], P('batch', 'mp')
- input_grad: float32 [32, 1024, 768], P('batch', 'mp')
- coeff_grad: float32 [32, 256, 768], P('batch', 'mp')
- first_gain_grad: float32 [768], replicated
- first_bias_grad: float32 [768], replicated
- query_key_value_matrix_grad: float32 [768, 3, 768], P(None, None, 'mp')
- qv_bias_grad: float32 [2, 768], P(None, 'mp')
- memory_weight_grad: float32 [2, 12, 256], P(None, 'mp')
- memory_bias_grad: float32 [2, 12], P(None, 'mp')
- output_matrix_grad: float32 [768, 768], P('mp')
- out_bias_grad: float32 [768], replicated
- second_gain_grad: float32 [768], replicated
- second_bias_grad: float32 [768], replicated
- up_weight_grad: float32 [768, 3072], P(None, 'mp')
- up_bias_grad: float32 [3072], P('mp')
- down_weight_grad: float32 [3072, 768], P('mp')
- down_bias_grad: float32 [768], replicated
Inputs may be any that keep to these rules, and one draw needn't show every extreme that they name: memory_flags holds one flag per sequence.
All inputs are finite; a program needn't handle non-finite values. No bound on the sum of `memory_flags` on one device may be relied on, other than what follows from the above.
Results may differ from a plain program's by a relative error of at most 0.013.
The roundings to bfloat16 on the way count: a program that leaves them out, or rounds other values in their place, can miss the bound.
Values may be sent and summed in bfloat16 or wider, within the bound.
No kernel may reach another device: no remote copies, remote signals or barrier semaphores. Data moves between devices by JAX's collectives and lax.ppermute only.
A program may use at most 320 MiB of HBM per device.

v0:
```python
import math

import jax
import jax.numpy as jnp
from jax import lax
from jax.sharding import PartitionSpec as P

HD = 64


def product(form, left_side, right_side):
    return jnp.einsum(form, left_side, right_side, precision=lax.Precision.HIGHEST)


def matrix_multiply(form, left_side, right_side):
    return jnp.einsum(form, left_side, right_side, preferred_element_type=jnp.float32)


def norm_parts(values, gain_vec, bias_vec):
    row_mean = jnp.mean(values, axis=-1, keepdims=True)
    centred = values - row_mean
    row_var = jnp.mean(centred * centred, axis=-1, keepdims=True)
    inverse = lax.rsqrt(row_var + 1e-05)
    scaled = centred * inverse
    return (scaled * gain_vec + bias_vec, scaled, inverse)


def norm_back(grad_out, scaled, inverse, gain_vec):
    grad_scaled = grad_out * gain_vec
    first_mean = jnp.mean(grad_scaled, axis=-1, keepdims=True)
    second_mean = jnp.mean(grad_scaled * scaled, axis=-1, keepdims=True)
    return inverse * (grad_scaled - first_mean - scaled * second_mean)


def basis_weights(memory_scores, weight_pair, bias_pair):
    basis_count = memory_scores.shape[-1]
    mean_logit = product("slhn,hn->slh", memory_scores, weight_pair[0]) + bias_pair[0]
    var_logit = product("slhn,hn->slh", memory_scores, weight_pair[1]) + bias_pair[1]
    centre = jax.nn.sigmoid(mean_logit)
    spread = 0.05 * jax.nn.softplus(var_logit) + (8.0 / basis_count) ** 2
    places = (jnp.arange(basis_count, dtype=jnp.float32) + 0.5) / basis_count
    offset = places - centre[..., None]
    return (
        jnp.exp(-offset * offset / (2.0 * spread[..., None]))
        * lax.rsqrt(2.0 * math.pi * spread[..., None])
        / basis_count
    )


def causal_scores(block_queries, key_rows, start_row, end_row):
    scores = matrix_multiply("sqhd,skhd->shqk", block_queries, key_rows[:, :end_row]) * 0.125
    allowed = jnp.arange(end_row)[None, :] <= jnp.arange(start_row, end_row)[:, None]
    return jnp.where(allowed, scores, -1e30)


def attend_forward(
    norm_output,
    coeffs,
    flag_vec,
    query_key_value_matrix,
    qv_bias,
    memory_weight,
    memory_bias,
    output_matrix,
):
    seq_count, length, model_width = norm_output.shape
    local_width = query_key_value_matrix.shape[2]
    head_count = local_width // HD
    basis_count = coeffs.shape[1]
    head_shape = (seq_count, length, head_count, HD)
    bias_values = qv_bias.astype(jnp.float32)
    projected_rows = matrix_multiply("zam,mwr->zawr", norm_output, query_key_value_matrix)
    queries = (projected_rows[:, :, 0] + bias_values[0]).astype(jnp.bfloat16).reshape(head_shape)
    key_rows = projected_rows[:, :, 1].astype(jnp.bfloat16).reshape(head_shape)
    values = (projected_rows[:, :, 2] + bias_values[1]).astype(jnp.bfloat16).reshape(head_shape)
    memory = matrix_multiply("snd,dcf->sncf", coeffs, query_key_value_matrix[:, 1:]).astype(
        jnp.bfloat16
    )
    memory_keys = memory[:, :, 0].reshape(seq_count, basis_count, head_count, HD)
    memory_values = memory[:, :, 1].reshape(seq_count, basis_count, head_count, HD)
    block_rows = min(512, length)
    attended_parts = []
    total_parts = []
    for block_index in range(length // block_rows):
        start_row = block_index * block_rows
        end_row = start_row + block_rows
        scores = causal_scores(queries[:, start_row:end_row], key_rows, start_row, end_row)
        top_score = jnp.max(scores, axis=-1, keepdims=True)
        raised = jnp.exp(scores - top_score)
        denominator = jnp.sum(raised, axis=-1, keepdims=True)
        weights = (raised / denominator).astype(jnp.bfloat16)
        attended_parts.append(matrix_multiply("shqk,skhd->sqhd", weights, values[:, :end_row]))
        total_parts.append(top_score[..., 0] + jnp.log(denominator[..., 0]))
    attended = jnp.concatenate(attended_parts, axis=1)
    log_totals = jnp.concatenate(total_parts, axis=2)
    memory_scores = matrix_multiply("slhd,snhd->slhn", queries, memory_keys) * 0.125
    basis_mass = basis_weights(
        memory_scores, memory_weight.astype(jnp.float32), memory_bias.astype(jnp.float32)
    ).astype(jnp.bfloat16)
    recalled = matrix_multiply("slhn,snhd->slhd", basis_mass, memory_values)
    flag_values = flag_vec.astype(jnp.float32)[:, None, None, None]
    combined_heads = (
        (attended + flag_values * recalled)
        .astype(jnp.bfloat16)
        .reshape(seq_count, length, local_width)
    )
    residual_piece = matrix_multiply("hom,mu->hou", combined_heads, output_matrix)
    kept = (
        queries,
        key_rows,
        values,
        memory_keys,
        memory_values,
        memory_scores,
        basis_mass,
        combined_heads,
        log_totals,
    )
    return (residual_piece, kept)


def attend_backward(
    residual_grad,
    norm_output,
    coeffs,
    flag_vec,
    query_key_value_matrix,
    memory_weight,
    memory_bias,
    output_matrix,
    kept,
):
    (
        queries,
        key_rows,
        values,
        memory_keys,
        memory_values,
        memory_scores,
        basis_mass,
        combined_heads,
        log_totals,
    ) = kept
    seq_count, length, model_width = norm_output.shape
    local_width = query_key_value_matrix.shape[2]
    head_count = local_width // HD
    basis_count = coeffs.shape[1]
    output_matrix_grad = matrix_multiply("qro,qrv->ov", combined_heads, residual_grad)
    combined_heads_grad = matrix_multiply("kpo,wo->kpw", residual_grad, output_matrix).astype(
        jnp.bfloat16
    )
    combined_heads_grad = combined_heads_grad.reshape(seq_count, length, head_count, HD)
    recalled_grad = combined_heads_grad * flag_vec[:, None, None, None]
    basis_grad = matrix_multiply("slhd,snhd->slhn", recalled_grad, memory_values)
    mvalues_grad = matrix_multiply("slhn,slhd->snhd", basis_mass, recalled_grad)
    unused_mass, pullback = jax.vjp(
        basis_weights,
        memory_scores,
        memory_weight.astype(jnp.float32),
        memory_bias.astype(jnp.float32),
    )
    scores_grad, memory_weight_grad, memory_bias_grad = pullback(basis_grad)
    scores_grad = scores_grad.astype(jnp.bfloat16)
    query_grad = matrix_multiply("slhn,snhd->slhd", scores_grad, memory_keys) * 0.125
    mkeys_grad = matrix_multiply("slhn,slhd->snhd", scores_grad, queries) * 0.125
    key_grad = jnp.zeros(key_rows.shape, jnp.float32)
    value_grad = jnp.zeros(values.shape, jnp.float32)
    block_rows = min(512, length)
    query_parts = []
    for block_index in range(length // block_rows):
        start_row = block_index * block_rows
        end_row = start_row + block_rows
        block_queries = queries[:, start_row:end_row]
        block_grad = combined_heads_grad[:, start_row:end_row]
        scores = causal_scores(block_queries, key_rows, start_row, end_row)
        weights = jnp.exp(scores - log_totals[:, :, start_row:end_row, None])
        weights_grad = matrix_multiply("sqhd,skhd->shqk", block_grad, values[:, :end_row])
        inner_sum = jnp.sum(weights * weights_grad, axis=-1, keepdims=True)
        block_scores_grad = (weights * (weights_grad - inner_sum)).astype(jnp.bfloat16)
        query_parts.append(
            matrix_multiply("shqk,skhd->sqhd", block_scores_grad, key_rows[:, :end_row]) * 0.125
        )
        key_grad = key_grad.at[:, :end_row].add(
            matrix_multiply("shqk,sqhd->skhd", block_scores_grad, block_queries) * 0.125
        )
        value_grad = value_grad.at[:, :end_row].add(
            matrix_multiply("shqk,sqhd->skhd", weights.astype(jnp.bfloat16), block_grad)
        )
    query_grad = query_grad + jnp.concatenate(query_parts, axis=1)
    query_key_value_rows_grad = jnp.stack([query_grad, key_grad, value_grad], axis=2).astype(
        jnp.bfloat16
    )
    query_key_value_rows_grad = query_key_value_rows_grad.reshape(seq_count, length, 3, local_width)
    memory_grads = jnp.stack([mkeys_grad, mvalues_grad], axis=2).astype(jnp.bfloat16)
    memory_grads = memory_grads.reshape(seq_count, basis_count, 2, local_width)
    query_key_value_matrix_grad = matrix_multiply(
        "arh,arkq->hkq", norm_output, query_key_value_rows_grad
    )
    query_key_value_matrix_grad = query_key_value_matrix_grad.at[:, 1:].add(
        matrix_multiply("snd,sncf->dcf", coeffs, memory_grads)
    )
    qv_bias_grad = jnp.sum(query_key_value_rows_grad[:, :, 0::2].astype(jnp.float32), axis=(0, 1))
    norm_output_grad = matrix_multiply(
        "zwev,oev->zwo", query_key_value_rows_grad, query_key_value_matrix
    )
    coeffs_grad = matrix_multiply("sncf,dcf->snd", memory_grads, query_key_value_matrix[:, 1:])
    return (
        norm_output_grad,
        coeffs_grad,
        query_key_value_matrix_grad,
        qv_bias_grad,
        memory_weight_grad,
        memory_bias_grad,
        output_matrix_grad,
    )


def feed_forward(norm_output, up_matrix, up_bias_vector, down_matrix):
    input_rows = matrix_multiply("ahg,gm->ahm", norm_output, up_matrix) + up_bias_vector.astype(
        jnp.float32
    )
    gelu_output = jax.nn.gelu(input_rows, approximate=True).astype(jnp.bfloat16)
    return (matrix_multiply("hom,mu->hou", gelu_output, down_matrix), input_rows, gelu_output)


def feed_backward(gradient_rows, norm_output, up_matrix, down_matrix, input_rows, gelu_output):
    down_output_grad = matrix_multiply("qro,qrv->ov", gelu_output, gradient_rows)
    hidden_state_grad = matrix_multiply("kpo,wo->kpw", gradient_rows, down_matrix)
    unused_value, pullback = jax.vjp(
        lambda inputs: jax.nn.gelu(inputs, approximate=True), input_rows
    )
    (input_rows_grad,) = pullback(hidden_state_grad)
    input_rows_grad = input_rows_grad.astype(jnp.bfloat16)
    up_output_grad = matrix_multiply("orx,ora->xa", norm_output, input_rows_grad)
    upb_grad = jnp.sum(input_rows_grad.astype(jnp.float32), axis=(0, 1))
    norm_output_grad = matrix_multiply("iqg,kg->iqk", input_rows_grad, up_matrix)
    return (norm_output_grad, up_output_grad, upb_grad, down_output_grad)


def per_device(
    hidden_in,
    memory_flags,
    memory_coeffs,
    first_gain,
    first_bias,
    query_key_value_matrix,
    qv_bias,
    memory_weight,
    memory_bias,
    output_matrix,
    out_bias,
    second_gain,
    second_bias,
    up_matrix,
    up_bias_vector,
    down_matrix,
    down_bias,
    out_grad,
):
    hidden = hidden_in.astype(jnp.float32)
    flag_local = memory_flags.astype(jnp.bfloat16)
    normed_one, scaled_one, inverse_one = norm_parts(hidden, first_gain, first_bias)
    normed_one = normed_one.astype(jnp.bfloat16)
    normed_all, coeffs_all = (
        lax.all_gather(normed_one, "mp", axis=1, tiled=True),
        lax.all_gather(memory_coeffs, "mp", axis=1, tiled=True),
    )
    residual_piece, kept = attend_forward(
        normed_all,
        coeffs_all,
        flag_local,
        query_key_value_matrix,
        qv_bias,
        memory_weight,
        memory_bias,
        output_matrix,
    )
    branch_total = lax.psum_scatter(residual_piece, "mp", scatter_dimension=1, tiled=True)
    middle = hidden + (branch_total + out_bias)
    normed_two, scaled_two, inverse_two = norm_parts(middle, second_gain, second_bias)
    normed_two_all = lax.all_gather(normed_two.astype(jnp.bfloat16), "mp", axis=1, tiled=True)
    feed_part, input_rows, gelu_output = feed_forward(
        normed_two_all, up_matrix, up_bias_vector, down_matrix
    )
    feed_total = lax.psum_scatter(
        feed_part.astype(jnp.bfloat16), "mp", scatter_dimension=1, tiled=True
    ).astype(jnp.float32)
    block_out = (middle + feed_total + down_bias).astype(jnp.bfloat16)
    grad_all = lax.all_gather(out_grad, "mp", axis=1, tiled=True)
    normed_two_part, up_output_grad, upb_grad, down_output_grad = feed_backward(
        grad_all, normed_two_all, up_matrix, down_matrix, input_rows, gelu_output
    )
    normed_two_grad = lax.psum_scatter(normed_two_part, "mp", scatter_dimension=1, tiled=True)
    out_grad_values = out_grad.astype(jnp.float32)
    middle_grad = out_grad_values + norm_back(normed_two_grad, scaled_two, inverse_two, second_gain)
    second_gain_grad = jnp.sum(normed_two_grad * scaled_two, axis=(0, 1))
    second_bias_grad = jnp.sum(normed_two_grad, axis=(0, 1))
    down_bias_grad = jnp.sum(out_grad_values, axis=(0, 1))
    residual_grad = middle_grad.astype(jnp.bfloat16)
    out_bias_grad = jnp.sum(residual_grad.astype(jnp.float32), axis=(0, 1))
    branch_grad_all = lax.all_gather(residual_grad, "mp", axis=1, tiled=True)
    normed_part, coeffs_part, qkv_grad, qv_grad, memw_grad, memb_grad, outw_grad = attend_backward(
        branch_grad_all,
        normed_all,
        coeffs_all,
        flag_local,
        query_key_value_matrix,
        memory_weight,
        memory_bias,
        output_matrix,
        kept,
    )
    normed_one_grad, coeff_grad = (
        lax.psum_scatter(
            normed_part.astype(jnp.bfloat16), "mp", scatter_dimension=1, tiled=True
        ).astype(jnp.float32),
        lax.psum_scatter(
            coeffs_part.astype(jnp.bfloat16), "mp", scatter_dimension=1, tiled=True
        ).astype(jnp.float32),
    )
    input_grad = middle_grad + norm_back(normed_one_grad, scaled_one, inverse_one, first_gain)
    first_gain_grad = jnp.sum(normed_one_grad * scaled_one, axis=(0, 1))
    first_bias_grad = jnp.sum(normed_one_grad, axis=(0, 1))
    (
        qkv_grad,
        qv_grad,
        memw_grad,
        memb_grad,
        outw_grad,
        up_output_grad,
        upb_grad,
        down_output_grad,
    ) = lax.psum(
        (
            qkv_grad,
            qv_grad,
            memw_grad,
            memb_grad,
            outw_grad,
            up_output_grad,
            upb_grad,
            down_output_grad,
        ),
        "batch",
    )
    (
        first_gain_grad,
        first_bias_grad,
        out_bias_grad,
        second_gain_grad,
        second_bias_grad,
        down_bias_grad,
    ) = lax.psum(
        (
            first_gain_grad,
            first_bias_grad,
            out_bias_grad,
            second_gain_grad,
            second_bias_grad,
            down_bias_grad,
        ),
        ("batch", "mp"),
    )
    return (
        block_out,
        input_grad,
        coeff_grad,
        first_gain_grad,
        first_bias_grad,
        qkv_grad,
        qv_grad,
        memw_grad,
        memb_grad,
        outw_grad,
        out_bias_grad,
        second_gain_grad,
        second_bias_grad,
        up_output_grad,
        upb_grad,
        down_output_grad,
        down_bias_grad,
    )


def solution(mesh):
    placed = (
        P("batch", "mp", None),
        P("batch"),
        P("batch", "mp", None),
        P(),
        P(),
        P(None, None, "mp"),
        P(None, "mp"),
        P(None, "mp", None),
        P(None, "mp"),
        P("mp", None),
        P(),
        P(),
        P(),
        P(None, "mp"),
        P("mp"),
        P("mp", None),
        P(),
        P("batch", "mp", None),
    )
    return jax.shard_map(
        per_device,
        mesh=mesh,
        in_specs=placed,
        out_specs=(
            P("batch", "mp", None),
            P("batch", "mp", None),
            P("batch", "mp", None),
            P(),
            P(),
            P(None, None, "mp"),
            P(None, "mp"),
            P(None, "mp", None),
            P(None, "mp"),
            P("mp", None),
            P(),
            P(),
            P(),
            P(None, "mp"),
            P("mp"),
            P("mp", None),
            P(),
        ),
        check_vma=False,
    )
```

profile of v0, /device:TPU:0, one launch (start us, length us, event | category | flops | bytes accessed | tf_op | source)
XLA Modules:
  0.0 850.8 jit_solution(11959987445198987662)
XLA Ops:
  9.2 2.1 fusion.67
  14.5 2.4 all_gather.16
  17.8 2.1 convolution_convert_fusion.1
  25.9 2.8 all-gather.5.cloned.1.call-done
  28.6 6.5 fusion.74
  36.5 2.5 fusion.193
  41.1 4.6 fusion.29
  45.7 4.3 fusion.31
  50.0 7.1 fusion.54
  57.1 10.7 %fusion.34 = (f32[2,6,512]{2,1,0:T(8,128)S(1)}, f32[2,6,512,1024]{3,2,1,0:T(8,128)}) fusion(pred[512,1024]{1,0:T(8,128)(4,1)S(1)} %iota_compare_fusion, bf16[2,1024,6,64]{1,3,2,0:T(8,128)(2,1)S(1)} %bitcast.292, bf16[2,1024,6,64]{1,3,2,0:T(8,128)(2,1)S(1)} %add_convert_fusion.3), kind=kOutput, calls=%fused_computation.57 | convolution fusion | flops 824174592 | bytes 28073984 | tf_op jit(solution)/shard_map/sqhd,skhd->shqk/dot_general | solution.py:16
  68.1 7.7 fusion.24
  75.9 7.7 fusion.98
  85.9 7.3 fusion
  93.3 8.5 %fusion.102 = f32[2,512,6,64]{1,3,2,0:T(8,128)} fusion(bf16[2,1024,6,64]{1,3,2,0:T(8,128)(2,1)S(1)} %add_convert_fusion.4, f32[2,6,512]{2,1,0:T(8,128)S(1)} %fusion, f32[2,6,512]{2,1,0:T(8,128)S(1)} %get-tuple-element.164, f32[2,6,512,1024]{3,2,1,0:T(8,128)S(1)} %bitcast.288, pred[512,1024]{1,0:T(8,128)(4,1)S(1)} %iota_compare_fusion), kind=kOutput, calls=%fused_computation.147 | convolution fusion | flops 836763648 | bytes 28884992 | tf_op jit(solution)/shard_map/shqk,skhd->sqhd/dot_general | solution.py:16
  102.8 16.8 %fusion.70 = bf16[2,1024,6,64]{1,3,2,0:T(8,128)(2,1)S(1)} fusion(f32[2,512,6,64]{1,3,2,0:T(8,128)} %fusion.102, f32[2,512,6,64]{1,3,2,0:T(8,128)} %fusion.98, bf16[2,256,6,64]{1,3,2,0:T(8,128)(2,1)S(1)} %bitcast.314, f32[2,1024,6]{1,2,0:T(8,128)S(1)} %get-tuple-element.149, f32[2,1024,6]{1,2,0:T(8,128)S(1)} %get-tuple-element.151, ...), kind=kOutput, calls=%fused_computation.105 | convolution fusion | flops 427819008 | bytes 5260296 | tf_op jit(solution)/shard_map/slhn,snhd->slhd/dot_general | solution.py:16
  120.8 4.4 fusion.140
  125.3 15.8 %reduce-scatter.6.cloned.1.call-done = f32[2,512,768]{2,1,0:T(8,128)} async-done(((f32[2,1024,768]{2,1,0:T(8,128)}), f32[2,512,768]{2,1,0:T(8,128)}) %reduce-scatter.6.cloned.1.call-update) | async-done | bytes 3145744 | tf_op jit(solution)/shard_map/reduce_scatter | solution.py:278
  141.1 2.9 fusion.192
  148.0 12.8 %all-gather.7.cloned.1.call-done = bf16[2,1024,768]{2,1,0:T(8,128)(2,1)} async-done(((bf16[2,512,768]{2,1,0:T(8,128)(2,1)}), bf16[2,1024,768]{2,1,0:T(8,128)(2,1)}) %all-gather.7.cloned.1.call-update) | async-done | bytes 3145744 | tf_op jit(solution)/shard_map/all_gather | solution.py:281
  160.8 13.4 %multiply_convert_fusion.2 = (bf16[2,1024,1536]{2,1,0:T(8,128)(2,1)}, f32[2,1024,1536]{2,1,0:T(8,128)}) fusion(f32[1536]{0:T(1024)S(1)} %convert_element_type.137, bf16[2,1024,768]{2,1,0:T(8,128)(2,1)} %all-gather.7.cloned.1.call-done, bf16[768,1536]{1,0:T(8,128)(2,1)S(1)} %copy-done), kind=kOutput, calls=%fused_computation.40 | convolution fusion | flops 4863295488 | bytes 24385536 | tf_op jit(solution)/shard_map/ahg,gm->ahm/dot_general | solution.py:16
  175.6 17.3 %convert_reduce_fusion = (f32[1536]{0:T(1024)}, bf16[2,1024,1536]{2,1,0:T(8,128)(2,1)S(1)}) fusion(f32[2,1024,1536]{2,1,0:T(8,128)} %get-tuple-element.171, f32[1536]{0:T(1024)S(1)} %convert_element_type.137, bf16[2,1024,768]{2,1,0:T(8,128)(2,1)} %all-gather.9.cloned.1.call-done, bf16[1536,768]{1,0:T(8,128)(2,1)} %param.47), kind=kOutput, calls=%fused_computation.34 | convolution fusion | flops 4904188416 | bytes 24391680 | tf_op jit(solution)/shard_map/kpo,wo->kpw/dot_general | solution.py:16
  192.9 2.7 copy-done.91
  195.6 6.9 fusion.82
  202.5 15.8 %reduce-scatter.10.cloned.1.call-done = f32[2,512,768]{2,1,0:T(8,128)} async-done(((f32[2,1024,768]{2,1,0:T(8,128)}), f32[2,512,768]{2,1,0:T(8,128)}) %reduce-scatter.10.cloned.1.call-update) | async-done | bytes 3145744 | tf_op jit(solution)/shard_map/reduce_scatter | solution.py:293
  218.3 4.7 multiply_reduce_fusion.2
  223.1 4.2 convert_reduce_fusion.5
  227.5 13.3 %all-gather.11.cloned.1.call-done = bf16[2,1024,768]{2,1,0:T(8,128)(2,1)} async-done(((bf16[2,512,768]{2,1,0:T(8,128)(2,1)}), bf16[2,1024,768]{2,1,0:T(8,128)(2,1)}) %all-gather.11.cloned.1.call-update) | async-done | bytes 3145744 | tf_op jit(solution)/shard_map/all_gather | solution.py:301
  240.8 3.4 convolution_convert_fusion
  244.3 8.0 fusion.99
  252.8 6.9 multiply_reduce_fusion.1
  259.6 7.1 multiply_convert_fusion.1
  266.8 3.2 multiply_bitcast_fusion.1
  270.0 2.4 multiply_bitcast_fusion.3
  272.4 4.1 fusion.112
  276.7 11.3 %fusion.6 = (f32[2,1024,6]{1,2,0:T(8,128)S(1)}, f32[2,1024,6]{1,2,0:T(8,128)S(1)}, f32[2,1024,6]{1,2,0:T(8,128)S(1)}) fusion(f32[2,1024,6]{1,2,0:T(8,128)S(1)} %copy-done.52, f32[2,1024,6]{1,2,0:T(8,128)S(1)} %copy-done.58, f32[256]{0:T(256)S(1)} %copy-done.90, f32[2,1024,6]{1,2,0:T(8,128)S(1)} %copy-done.54, f32[2,1024,6]{1,2,0:T(8,128)S(1)} %get-tuple-element.148, ...), kind=kOutput, calls=%fused_computation.17 | convolution fusion | flops 460025856 | bytes 2311172 | tf_op jit(solution)/shard_map/slhd,snhd->slhn/dot_general | solution.py:16
  288.3 5.3 fusion.109
  294.9 3.0 bitcast_convert_fusion.1
  298.0 18.1 %multiply_reduce_fusion = (f32[2,6,512]{2,1,0:T(8,128)S(1)}, f32[2,6,512,1024]{3,2,1,0:T(8,128)}) fusion(f32[2,6,512]{2,1,0:T(8,128)S(1)} %log_add_fusion, f32[2,6,512,1024]{3,2,1,0:T(8,128)} %get-tuple-element.165, pred[512,1024]{1,0:T(8,128)(4,1)S(1)} %copy-done.8, bf16[2,1024,6,64]{1,3,2,0:T(8,128)(2,1)} %copy-done.16, bf16[2,1024,6,64]{1,3,2,0:T(8,128)(2,1)} %bitcast.312), kind=kOutput, calls=%fused_computation.1 | convolution fusion | flops 836757504 | bytes 53264384 | tf_op jit(solution)/shard_map/sqhd,skhd->shqk/dot_general | solution.py:16
  316.1 13.5 %fusion.76 = bf16[2,1024,6,64]{1,3,2,0:T(8,128)(2,1)} fusion(f32[2,512,6,64]{1,3,2,0:T(8,128)} %fusion.99, f32[2,6,512]{2,1,0:T(8,128)S(1)} %log_add_fusion, f32[2,6,512,1024]{3,2,1,0:T(8,128)} %get-tuple-element.165, pred[512,1024]{1,0:T(8,128)(4,1)S(1)} %copy-done.8, bf16[2,1024,6,64]{1,3,2,0:T(8,128)(2,1)} %bitcast.313), kind=kOutput, calls=%fused_computation.113 | convolution fusion | flops 832045056 | bytes 29646848 | tf_op jit(solution)/shard_map/shqk,sqhd->skhd/dot_general | solution.py:16
  329.5 2.6 copy.71
  332.1 21.4 %multiply_convert_fusion = bf16[2,6,512,1024]{3,2,1,0:T(8,128)(2,1)} fusion(f32[2,6,512,1024]{3,2,1,0:T(8,128)} %get-tuple-element.169, f32[2,6,512]{2,1,0:T(8,128)S(1)} %get-tuple-element.168, f32[2,6,512]{2,1,0:T(8,128)S(1)} %log_add_fusion, f32[2,6,512,1024]{3,2,1,0:T(8,128)} %get-tuple-element.165, pred[512,1024]{1,0:T(8,128)(4,1)S(1)} %copy-done.8), kind=kLoop, calls=%fused_computation | loop fusion | flops 37748736 | bytes 63488000 | tf_op jit(solution)/shard_map/convert_element_type | solution.py:179
  353.5 8.6 %multiply_bitcast_fusion.2 = f32[2,512,6,64]{1,3,2,0:T(8,128)S(1)} fusion(bf16[2,1024,6,64]{1,3,2,0:T(8,128)(2,1)S(1)} %bitcast.294, bf16[2,6,512,1024]{3,2,1,0:T(8,128)(2,1)} %multiply_convert_fusion), kind=kOutput, calls=%fused_computation.143 | convolution fusion | flops 805699584 | bytes 15728640 | tf_op jit(solution)/shard_map/shqk,skhd->sqhd/dot_general | solution.py:16
  362.2 5.9 fusion.71
  368.1 2.6 copy.69
  370.6 8.4 fusion.77
  379.1 2.7 copy.70
  381.8 8.4 bitcast_convert_fusion
  390.3 9.0 %fusion.86 = bf16[2,1024,768]{2,1,0:T(8,128)(2,1)} fusion(bf16[2,1024,1536]{2,1,0:T(8,128)(2,1)} %get-tuple-element.170, bf16[1536,768]{1,0:T(8,128)(2,1)} %param.47), kind=kOutput, calls=%fused_computation.135 | convolution fusion | flops 4833411072 | bytes 11796480 | tf_op jit(solution)/shard_map/hom,mu->hou/dot_general | solution.py:16
  399.4 10.4 %convolution_bitcast_fusion.1 = f32[768,1536]{1,0:T(8,128)} fusion(bf16[2,1024,768]{2,1,0:T(8,128)(2,1)} %all-gather.7.cloned.1.call-done, bf16[2,1024,1536]{2,1,0:T(8,128)(2,1)} %copy-done.91), kind=kOutput, calls=%fused_computation.90 | convolution fusion | flops 4831838208 | bytes 14155776 | tf_op jit(solution)/shard_map/orx,ora->xa/dot_general | solution.py:16
  409.7 8.9 %convolution_bitcast_fusion = f32[1536,768]{1,0:T(8,128)} fusion(bf16[2,1024,1536]{2,1,0:T(8,128)(2,1)} %get-tuple-element.170, bf16[2,1024,768]{2,1,0:T(8,128)(2,1)S(1)} %copy-done.85), kind=kOutput, calls=%fused_computation.89 | convolution fusion | flops 4831838208 | bytes 14155776 | tf_op jit(solution)/shard_map/qro,qrv->ov/dot_general | solution.py:16
  418.6 6.1 fusion.89
  424.7 4.0 fusion.78
  428.8 2.4 convolution_bitcast_fusion.2
  432.0 13.3 %fusion.27 = f32[6,1,256,1]{2,1,3,0:T(1,128)S(1)} fusion(f32[2,1024,6,256]{1,3,2,0:T(8,128)} %copy-done.2, f32[6,2,1024,1]{2,0,1,3:T(8,128)S(1)} %bitcast.319), kind=kOutput, calls=%fused_computation.50 | convolution fusion | flops 37748736 | bytes 12638208 | tf_op jit(solution)/shard_map/transpose(jvp(slhn,hn->slh))/dot_general | solution.py:12
  445.4 13.4 %fusion.25 = f32[6,1,256,1]{2,1,3,0:T(1,128)S(1)} fusion(f32[2,1024,6,256]{1,3,2,0:T(8,128)} %copy-done.2, f32[6,2,1024,1]{2,0,1,3:T(8,128)S(1)} %bitcast.318), kind=kOutput, calls=%fused_computation.48 | convolution fusion | flops 37748736 | bytes 12638208 | tf_op jit(solution)/shard_map/transpose(jvp(slhn,hn->slh))/dot_general | solution.py:12
  460.5 81.6 %all-reduce.7 = (f32[2,384]{1,0:T(2,128)}, f32[2,6,256]{2,1,0:T(8,128)S(1)}, f32[2,6]{1,0:T(2,128)}, f32[1536]{0:T(1024)}) all-reduce(f32[2,384]{1,0:T(2,128)S(1)} %convert_reduce_fusion.1, f32[2,6,256]{2,1,0:T(8,128)S(1)} %pad_add_fusion, f32[2,6]{1,0:T(2,128)S(1)} %pad_add_fusion.1, ...), channel_id=1, replica_groups=mesh['batch'=16,'mp'=2] {'batch'}, use_global_device_ids=true, to_apply=%region_28.29 | all-reduce | flops 5388 | bytes 43104 | tf_op jit(solution)/shard_map/psum | solution.py:333
  542.8 2.0 convert_element_type.155
  544.7 2.8 fusion.69
  547.7 8.3 fusion.66
  556.0 40.4 %all-reduce.6 = (f32[768]{0:T(1024)}, f32[768]{0:T(1024)}, f32[768]{0:T(1024)}, f32[768]{0:T(1024)}, f32[768]{0:T(1024)}, /*index=5*/f32[768]{0:T(1024)}) all-reduce(f32[768]{0:T(1024)S(1)} %get-tuple-element.115, f32[768]{0:T(1024)S(1)} %get-tuple-element.120, ...), channel_id=1, replica_groups=mesh['batch'=16,'mp'=2] {'batch','mp'}, use_global_device_ids=true, to_apply=%region_23.24 | all-reduce | flops 4608 | bytes 36864 | tf_op jit(solution)/shard_map/psum | solution.py:353
  596.4 236.2 %all-reduce.11.cloned.1.call-done = (f32[768,3,384]{2,0,1:T(8,128)}, f32[384,768]{1,0:T(8,128)}, f32[768,1536]{1,0:T(8,128)}, f32[1536,768]{1,0:T(8,128)}) async-done(((f32[768,3,384]{2,0,1:T(8,128)}, f32[384,768]{1,0:T(8,128)}, f32[768,1536]{1,0:T(8,128)}, f32[1536,768]{1,0:T(8,128)}), (f32[768,3,384]{2,0,1:T(8,128)}, f32[384,768]{1,0:T(8,128)}, f32[768,1536]{1,0:T(8,128)}, ...) | async-done | bytes 14155792 | tf_op jit(solution)/shard_map/psum | solution.py:333
  832.7 4.2 copy.187
  837.9 2.4 copy.189
  841.3 2.2 copy.190
  (287 shorter events, 33.2 us)
Async XLA Ops:
  7.2 153.6 %copy-start = (bf16[768,1536]{1,0:T(8,128)(2,1)S(1)}, bf16[768,1536]{1,0:T(8,128)(2,1)}, u32[]{:S(2)}) copy-start(bf16[768,1536]{1,0:T(8,128)(2,1)} %param.45) | copy-start | bytes 7077892
  7.2 21.4 %all-gather.5.cloned.1.call-start = ((), (), s32[]{:S(2)}) async-start(), calls=%async_computation.5 | async-start | bytes 4718592 | tf_op jit(solution)/shard_map/all_gather | solution.py:265
  13.7 127.4 %reduce-scatter.6.cloned.1.call-start = ((), (), s32[]{:S(2)}) async-start(), calls=%async_computation.6 | async-start | bytes 9437184 | tf_op jit(solution)/shard_map/reduce_scatter | solution.py:278
  20.1 19.1 %copy-start.30 = (bf16[2,256,1,384]{1,3,0,2:T(8,128)(2,1)}, bf16[2,256,1,384]{1,3,0,2:T(8,128)(2,1)S(1)}, u32[]{:S(2)}) copy-start(bf16[2,256,1,384]{1,3,0,2:T(8,128)(2,1)S(1)} %copy.61) | copy-start | bytes 1179652
  21.7 54.1 %copy-start.18 = (pred[512,512]{0,1:T(8,128)(4,1)}, pred[512,512]{0,1:T(8,128)(4,1)S(1)}, u32[]{:S(2)}) copy-start(pred[512,512]{0,1:T(8,128)(4,1)S(1)} %iota_compare_fusion.1) | copy-start | bytes 786436
  25.9 67.4 %copy-start.7 = (pred[512,1024]{1,0:T(8,128)(4,1)}, pred[512,1024]{1,0:T(8,128)(4,1)S(1)}, u32[]{:S(2)}) copy-start(pred[512,1024]{1,0:T(8,128)(4,1)S(1)} %iota_compare_fusion) | copy-start | bytes 1572868
  39.3 17.9 %copy-start.9 = (bf16[2,1024,6,64]{1,3,2,0:T(8,128)(2,1)}, bf16[2,1024,6,64]{1,3,2,0:T(8,128)(2,1)S(1)}, u32[]{:S(2)}) copy-start(bf16[2,1024,6,64]{1,3,2,0:T(8,128)(2,1)S(1)} %add_convert_fusion.3) | copy-start | bytes 4718596
  45.7 56.3 %copy-start.34 = (f32[6,1,2,1024]{3,1,2,0:T(1,128)}, f32[6,1,2,1024]{3,1,2,0:T(1,128)S(1)}, u32[]{:S(2)}) copy-start(f32[6,1,2,1024]{3,1,2,0:T(1,128)S(1)} %fusion.29) | copy-start | bytes 147460
  50.0 51.9 %copy-start.36 = (f32[6,1,2,1024]{3,1,2,0:T(1,128)}, f32[6,1,2,1024]{3,1,2,0:T(1,128)S(1)}, u32[]{:S(2)}) copy-start(f32[6,1,2,1024]{3,1,2,0:T(1,128)S(1)} %fusion.31) | copy-start | bytes 147460
  57.1 10.7 %copy-start.15 = (f32[2,1024,1,384]{1,3,2,0:T(8,128)S(1)}, f32[2,1024,1,384]{1,3,2,0:T(8,128)}, u32[]{:S(2)}) copy-start(f32[2,1024,1,384]{1,3,2,0:T(8,128)} %get-tuple-element.142) | copy-start | bytes 9437188
  68.1 25.2 %copy-start.16 = (bf16[2,1024,6,64]{1,3,2,0:T(8,128)(2,1)}, bf16[2,1024,6,64]{1,3,2,0:T(8,128)(2,1)S(1)}, u32[]{:S(2)}) copy-start(bf16[2,1024,6,64]{1,3,2,0:T(8,128)(2,1)S(1)} %add_convert_fusion.4) | copy-start | bytes 4718596
  68.1 15.5 %slice-start = ((s8[25165824]{0:T(1024)(128)(4,1)}), s8[4194304]{0:T(1024)(128)(4,1)S(1)}, s32[]{:S(2)}) async-start(s8[25165824]{0:T(1024)(128)(4,1)} %bitcast.287), calls=%async_computation.15 | async-start | bytes 8388608
  68.1 15.5 %slice-start.1 = ((s8[25165824]{0:T(1024)(128)(4,1)}), s8[4194304]{0:T(1024)(128)(4,1)S(1)}, s32[]{:S(2)}) async-start(s8[25165824]{0:T(1024)(128)(4,1)} %bitcast.287), calls=%async_computation.16 | async-start | bytes 8388608
  75.9 8.8 %slice-start.4 = ((s8[25165824]{0:T(1024)(128)(4,1)}), s8[4194304]{0:T(1024)(128)(4,1)S(1)}, s32[]{:S(2)}) async-start(s8[25165824]{0:T(1024)(128)(4,1)} %bitcast.287), calls=%async_computation.19 | async-start | bytes 8388608
  75.9 10.0 %slice-start.5 = ((s8[25165824]{0:T(1024)(128)(4,1)}), s8[4194304]{0:T(1024)(128)(4,1)S(1)}, s32[]{:S(2)}) async-start(s8[25165824]{0:T(1024)(128)(4,1)} %bitcast.287), calls=%async_computation.20 | async-start | bytes 8388608
  93.3 8.7 %copy-start.73 = (f32[6]{0:T(128)S(1)}, f32[6]{0:T(128)}, u32[]{:S(2)}) copy-start(f32[6]{0:T(128)} %get-tuple-element.159) | copy-start | bytes 76
  93.3 9.5 %copy-start.39 = (bf16[2,256,1,384]{1,3,0,2:T(8,128)(2,1)S(1)}, bf16[2,256,1,384]{1,3,0,2:T(8,128)(2,1)}, u32[]{:S(2)}) copy-start(bf16[2,256,1,384]{1,3,0,2:T(8,128)(2,1)} %copy.60) | copy-start | bytes 1179652
  93.3 9.5 %copy-start.89 = (f32[2]{0:T(128)S(1)}, f32[2]{0:T(128)}, u32[]{:S(2)}) copy-start(f32[2]{0:T(128)} %get-tuple-element.161) | copy-start | bytes 28
  93.3 9.5 %copy-start.90 = (f32[256]{0:T(256)S(1)}, f32[256]{0:T(256)}, u32[]{:S(2)}) copy-start(f32[256]{0:T(256)} %add_multiply_fusion) | copy-start | bytes 3076
  102.0 17.6 %copy-start.57 = (f32[2,1024,6]{1,2,0:T(8,128)}, f32[2,1024,6]{1,2,0:T(8,128)S(1)}, u32[]{:S(2)}) copy-start(f32[2,1024,6]{1,2,0:T(8,128)S(1)} %fusion.189) | copy-start | bytes 147460
  102.8 16.8 %copy-start.53 = (f32[2,1024,6]{1,2,0:T(8,128)}, f32[2,1024,6]{1,2,0:T(8,128)S(1)}, u32[]{:S(2)}) copy-start(f32[2,1024,6]{1,2,0:T(8,128)S(1)} %get-tuple-element.151) | copy-start | bytes 147460
  102.8 16.8 %copy-start.55 = (f32[2,1024,6]{1,2,0:T(8,128)}, f32[2,1024,6]{1,2,0:T(8,128)S(1)}, u32[]{:S(2)}) copy-start(f32[2,1024,6]{1,2,0:T(8,128)S(1)} %get-tuple-element.149) | copy-start | bytes 147460
  102.8 18.0 %copy-start.38 = (bf16[384,768]{1,0:T(8,128)(2,1)S(1)}, bf16[384,768]{1,0:T(8,128)(2,1)}, u32[]{:S(2)}) copy-start(bf16[384,768]{1,0:T(8,128)(2,1)} %param.41) | copy-start | bytes 1769476
  125.2 15.9 %copy-start.79 = (f32[768]{0:T(1024)S(1)}, f32[768]{0:T(1024)}, u32[]{:S(2)}) copy-start(f32[768]{0:T(1024)} %param.42) | copy-start | bytes 9220
  125.2 35.6 %all-gather.7.cloned.1.call-start = ((), (), s32[]{:S(2)}) async-start(), calls=%async_computation.7 | async-start | bytes 4718592 | tf_op jit(solution)/shard_map/all_gather | solution.py:281
  144.0 79.1 %copy-start.44 = (f32[2,512]{1,0:T(2,128)}, f32[2,512]{1,0:T(2,128)S(1)}, u32[]{:S(2)}) copy-start(f32[2,512]{1,0:T(2,128)S(1)} %broadcast_multiply_fusion.6) | copy-start | bytes 12292
  145.6 77.4 %copy-start.48 = (f32[2,512]{1,0:T(2,128)}, f32[2,512]{1,0:T(2,128)S(1)}, u32[]{:S(2)}) copy-start(f32[2,512]{1,0:T(2,128)S(1)} %add_rsqrt_fusion) | copy-start | bytes 12292
  147.3 28.2 %all-gather.9.cloned.1.call-start = ((), (), s32[]{:S(2)}) async-start(), calls=%async_computation.9 | async-start | bytes 4718592 | tf_op jit(solution)/shard_map/all_gather | solution.py:289
  147.9 70.4 %reduce-scatter.10.cloned.1.call-start = ((), (), s32[]{:S(2)}) async-start(), calls=%async_computation.10 | async-start | bytes 9437184 | tf_op jit(solution)/shard_map/reduce_scatter | solution.py:293
  202.5 20.6 %copy-start.14 = (bf16[2,512,768]{2,1,0:T(8,128)(2,1)S(1)}, bf16[2,512,768]{2,1,0:T(8,128)(2,1)}, u32[]{:S(2)}) copy-start(bf16[2,512,768]{2,1,0:T(8,128)(2,1)} %param.49) | copy-start | bytes 4718596
  202.5 38.3 %all-gather.11.cloned.1.call-start = ((), (), s32[]{:S(2)}) async-start(), calls=%async_computation.11 | async-start | bytes 4718592 | tf_op jit(solution)/shard_map/all_gather | solution.py:301
  227.4 315.4 %reduce-scatter.14.cloned.1.call-start = ((), (), s32[]{:S(2)}) async-start(), calls=%async_computation.13 | async-start | bytes 1179648 | tf_op jit(solution)/shard_map/reduce_scatter | solution.py:317
  227.5 16.8 %copy-start.19 = (pred[512,512]{0,1:T(8,128)(4,1)S(1)}, pred[512,512]{0,1:T(8,128)(4,1)}, u32[]{:S(2)}) copy-start(pred[512,512]{0,1:T(8,128)(4,1)} %copy-done.18) | copy-start | bytes 786436
  240.8 11.5 %slice-start.6 = ((s8[12582912]{0:T(1024)(128)(4,1)}), s8[4194304]{0:T(1024)(128)(4,1)S(1)}, s32[]{:S(2)}) async-start(s8[12582912]{0:T(1024)(128)(4,1)} %bitcast.289), calls=%async_computation.21 | async-start | bytes 8388608
  244.3 28.1 %copy-start.32 = (bf16[2,1024,384]{1,2,0:T(8,128)(2,1)}, bf16[2,1024,384]{1,2,0:T(8,128)(2,1)S(1)}, u32[]{:S(2)}) copy-start(bf16[2,1024,384]{1,2,0:T(8,128)(2,1)S(1)} %convolution_convert_fusion) | copy-start | bytes 4718596
  276.7 11.4 %copy-start.35 = (f32[6,1,2,1024]{3,1,2,0:T(1,128)S(1)}, f32[6,1,2,1024]{3,1,2,0:T(1,128)}, u32[]{:S(2)}) copy-start(f32[6,1,2,1024]{3,1,2,0:T(1,128)} %copy-done.34) | copy-start | bytes 147460
  276.7 11.4 %copy-start.37 = (f32[6,1,2,1024]{3,1,2,0:T(1,128)S(1)}, f32[6,1,2,1024]{3,1,2,0:T(1,128)}, u32[]{:S(2)}) copy-start(f32[6,1,2,1024]{3,1,2,0:T(1,128)} %copy-done.36) | copy-start | bytes 147460
  276.7 11.4 %copy-start.72 = (f32[6]{0:T(128)S(1)}, f32[6]{0:T(128)}, u32[]{:S(2)}) copy-start(f32[6]{0:T(128)} %get-tuple-element.158) | copy-start | bytes 76
  276.7 11.4 %copy-start.74 = (f32[6]{0:T(128)S(1)}, f32[6]{0:T(128)}, u32[]{:S(2)}) copy-start(f32[6]{0:T(128)} %get-tuple-element.159) | copy-start | bytes 76
  276.7 11.6 %copy-start.76 = (f32[6,256]{1,0:T(8,128)S(1)}, f32[6,256]{1,0:T(8,128)}, u32[]{:S(2)}) copy-start(f32[6,256]{1,0:T(8,128)} %get-tuple-element.154) | copy-start | bytes 18436
  276.7 11.6 %copy-start.77 = (f32[6,256]{1,0:T(8,128)S(1)}, f32[6,256]{1,0:T(8,128)}, u32[]{:S(2)}) copy-start(f32[6,256]{1,0:T(8,128)} %get-tuple-element.152) | copy-start | bytes 18436
  288.3 73.9 %copy-start.42 = (f32[6,2,1024]{2,0,1:T(8,128)}, f32[6,2,1024]{2,0,1:T(8,128)S(1)}, u32[]{:S(2)}) copy-start(f32[6,2,1024]{2,0,1:T(8,128)S(1)} %get-tuple-element.174) | copy-start | bytes 147460
  297.9 246.8 %reduce-scatter.12.cloned.1.call-start = ((), (), s32[]{:S(2)}) async-start(), calls=%async_computation.12 | async-start | bytes 4718592 | tf_op jit(solution)/shard_map/reduce_scatter | solution.py:314
  332.1 21.4 %copy-start.13 = (bf16[2,1024,1,384]{1,3,2,0:T(8,128)(2,1)S(1)}, bf16[2,1024,1,384]{1,3,2,0:T(8,128)(2,1)}, u32[]{:S(2)}) copy-start(bf16[2,1024,1,384]{1,3,2,0:T(8,128)(2,1)} %slice.267) | copy-start | bytes 4718596
  353.5 8.7 %copy-start.29 = (f32[2,512,6,64]{1,3,2,0:T(8,128)S(1)}, f32[2,512,6,64]{1,3,2,0:T(8,128)}, u32[]{:S(2)}) copy-start(f32[2,512,6,64]{1,3,2,0:T(8,128)} %multiply_bitcast_fusion.3) | copy-start | bytes 4718596
  353.5 8.7 %copy-start.31 = (bf16[2,256,1,384]{1,3,0,2:T(8,128)(2,1)S(1)}, bf16[2,256,1,384]{1,3,0,2:T(8,128)(2,1)}, u32[]{:S(2)}) copy-start(bf16[2,256,1,384]{1,3,0,2:T(8,128)(2,1)} %copy-done.30) | copy-start | bytes 1179652
  390.2 157.4 %reduce-scatter.8.cloned.1.call-start = ((), (), s32[]{:S(2)}) async-start(), calls=%async_computation.8 | async-start | bytes 4718592 | tf_op jit(solution)/shard_map/reduce_scatter | solution.py:285
  399.3 433.3 %all-reduce.11.cloned.1.call-start = ((), (), s32[]{:S(2)}) async-start(), calls=%async_computation.14 | async-start | bytes 28311552 | tf_op jit(solution)/shard_map/psum | solution.py:333
  399.4 10.4 %copy-start.85 = (bf16[2,1024,768]{2,1,0:T(8,128)(2,1)S(1)}, bf16[2,1024,768]{2,1,0:T(8,128)(2,1)}, u32[]{:S(2)}) copy-start(bf16[2,1024,768]{2,1,0:T(8,128)(2,1)} %all-gather.9.cloned.1.call-done) | copy-start | bytes 9437188
  409.7 8.9 %copy-start.21 = (bf16[2,1024,1,384]{3,1,2,0:T(8,128)(2,1)S(1)}, bf16[2,1024,1,384]{3,1,2,0:T(8,128)(2,1)}, u32[]{:S(2)}) copy-start(bf16[2,1024,1,384]{3,1,2,0:T(8,128)(2,1)} %copy.69) | copy-start | bytes 4718596
  409.7 8.9 %copy-start.23 = (bf16[2,1024,1,384]{3,1,2,0:T(8,128)(2,1)S(1)}, bf16[2,1024,1,384]{3,1,2,0:T(8,128)(2,1)}, u32[]{:S(2)}) copy-start(bf16[2,1024,1,384]{3,1,2,0:T(8,128)(2,1)} %copy.70) | copy-start | bytes 4718596
  409.7 8.9 %copy-start.84 = (bf16[2,1024,768]{2,1,0:T(8,128)(2,1)S(1)}, bf16[2,1024,768]{2,1,0:T(8,128)(2,1)}, u32[]{:S(2)}) copy-start(bf16[2,1024,768]{2,1,0:T(8,128)(2,1)} %all-gather.5.cloned.1.call-done) | copy-start | bytes 9437188
  445.4 13.7 %copy-start.22 = (bf16[2,1024,1,384]{3,1,2,0:T(8,128)(2,1)S(1)}, bf16[2,1024,1,384]{3,1,2,0:T(8,128)(2,1)}, u32[]{:S(2)}) copy-start(bf16[2,1024,1,384]{3,1,2,0:T(8,128)(2,1)} %copy.69) | copy-start | bytes 4718596
  445.4 13.7 %copy-start.24 = (bf16[2,1024,1,384]{3,1,2,0:T(8,128)(2,1)S(1)}, bf16[2,1024,1,384]{3,1,2,0:T(8,128)(2,1)}, u32[]{:S(2)}) copy-start(bf16[2,1024,1,384]{3,1,2,0:T(8,128)(2,1)} %copy.70) | copy-start | bytes 4718596
  459.8 84.9 %copy-start.5 = (bf16[2,512,768]{2,1,0:T(8,128)(2,1)S(1)}, bf16[2,512,768]{2,1,0:T(8,128)(2,1)}, u32[]{:S(2)}) copy-start(bf16[2,512,768]{2,1,0:T(8,128)(2,1)} %param.32) | copy-start | bytes 4718596
  459.8 84.9 %copy-start.47 = (f32[2,512]{1,0:T(2,128)S(1)}, f32[2,512]{1,0:T(2,128)}, u32[]{:S(2)}) copy-start(f32[2,512]{1,0:T(2,128)} %copy-done.46) | copy-start | bytes 12292
  459.8 84.9 %copy-start.51 = (f32[2,512]{1,0:T(2,128)S(1)}, f32[2,512]{1,0:T(2,128)}, u32[]{:S(2)}) copy-start(f32[2,512]{1,0:T(2,128)} %copy-done.50) | copy-start | bytes 12292
  459.9 84.9 %copy-start.62 = (f32[768]{0:T(1024)S(1)}, f32[768]{0:T(1024)}, u32[]{:S(2)}) copy-start(f32[768]{0:T(1024)} %param.35) | copy-start | bytes 9220
  459.9 87.7 %copy-start.45 = (f32[2,512]{1,0:T(2,128)S(1)}, f32[2,512]{1,0:T(2,128)}, u32[]{:S(2)}) copy-start(f32[2,512]{1,0:T(2,128)} %copy-done.44) | copy-start | bytes 12292
  459.9 87.7 %copy-start.49 = (f32[2,512]{1,0:T(2,128)S(1)}, f32[2,512]{1,0:T(2,128)}, u32[]{:S(2)}) copy-start(f32[2,512]{1,0:T(2,128)} %copy-done.48) | copy-start | bytes 12292
  459.9 87.7 %copy-start.60 = (f32[768]{0:T(1024)S(1)}, f32[768]{0:T(1024)}, u32[]{:S(2)}) copy-start(f32[768]{0:T(1024)} %param.43) | copy-start | bytes 9220
  459.9 87.7 %copy-start.64 = (f32[2,512]{1,0:T(2,128)S(1)}, f32[2,512]{1,0:T(2,128)}, u32[]{:S(2)}) copy-start(f32[2,512]{1,0:T(2,128)} %copy-done.63) | copy-start | bytes 12292
  459.9 87.7 %copy-start.66 = (f32[2,512]{1,0:T(2,128)S(1)}, f32[2,512]{1,0:T(2,128)}, u32[]{:S(2)}) copy-start(f32[2,512]{1,0:T(2,128)} %copy-done.65) | copy-start | bytes 12292
  459.9 87.7 %copy-start.81 = (f32[768]{0:T(1024)S(1)}, f32[768]{0:T(1024)}, u32[]{:S(2)}) copy-start(f32[768]{0:T(1024)} %param.48) | copy-start | bytes 9220
  (51 other events, 228.0 us)
Sparse Core Ops, SparseCore 0:
  13.8 14.8 all-gather.4
  125.3 15.6 reduce-scatter.5
  147.5 13.2 all-gather.6
  162.3 13.2 all-gather.8
  202.6 15.6 reduce-scatter.9
  227.5 13.2 all-gather.10
  298.0 9.4 reduce-scatter.13
  390.3 12.0 reduce-scatter.11
  404.7 12.0 reduce-scatter.7
  431.3 401.2 all-reduce.10
where the time goes:
time: 861 us; the launch traced here: 851 us
  waiting for transfers between devices  299 us (35%)
  matrix products  290 us (34%)
  blocking collectives  125 us (15%)
  other arithmetic  83.4 us (10%)
  local copies, waits for them, and re-layouts  37.8 us (4%)
  between operations  15.9 us (2%)
    dot_general x33, matrix products, matrix_multiply(): jnp.einsum(form, left_side, right_side, preferred_element_type=jnp.float32)  254 us
    psum x1, waiting for transfers between devices, per_device(): lax.psum((qkv_grad, qv_grad, memw_grad, memb_grad, outw_grad, up_output_g...  236 us
    psum x1, blocking collectives, per_device(): lax.psum((qkv_grad, qv_grad, memw_grad, memb_grad, outw_grad, up_output_g...  81.6 us
    psum x1, blocking collectives, per_device(): lax.psum((first_gain_grad, first_bias_grad, out_bias_grad, second_gain_gr...  40.4 us
    dot_general x4, matrix products, product(): jnp.einsum(form, left_side, right_side, precision=lax.Precision.HIGHEST)  35.6 us
    convert_element_type x2, other arithmetic, attend_backward(): (weights * (weights_grad - inner_sum)).astype(jnp.bfloat16)  28.5 us
    unnamed x215, local copies, waits for them, and re-layouts  21.9 us
  transfers between devices with their start and end apart: 10, of which 7 were waited for; matrix products, arithmetic and copies ran while one was open for 23% of the time, Pallas kernels for 0%

commit v1 on v0

v1 whole, which is shorter than its diff:
```python
import functools
import math

import jax
import jax.numpy as jnp
from jax import lax
from jax.experimental import pallas as pl
from jax.experimental.pallas import tpu as pltpu
from jax.sharding import PartitionSpec as P

HD = 64
BLOCK = 256
BF16 = jnp.bfloat16
F32 = jnp.float32
VMEM_BYTES = 56 * 2**20


def dot_nn(left, right):
    return lax.dot_general(left, right, (((1,), (0,)), ((), ())), preferred_element_type=F32)


def dot_nt(left, right):
    return lax.dot_general(left, right, (((1,), (1,)), ((), ())), preferred_element_type=F32)


def dot_tn(left, right):
    return lax.dot_general(left, right, (((0,), (0,)), ((), ())), preferred_element_type=F32)


def dot_tn_exact(left, right):
    return lax.dot_general(
        left,
        right,
        (((0,), (0,)), ((), ())),
        precision=lax.Precision.HIGHEST,
        preferred_element_type=F32,
    )


def three_parts(values):
    high = values.astype(BF16).astype(F32)
    rest = values - high
    middle = rest.astype(BF16).astype(F32)
    return jnp.concatenate([high, middle, rest - middle], axis=0).astype(BF16)


def add_parts(stacked):
    rows = stacked.shape[0] // 3
    return stacked[:rows] + stacked[rows : 2 * rows] + stacked[2 * rows :]


def scaled_rows(values):
    row_mean = jnp.mean(values, axis=-1, keepdims=True)
    centred = values - row_mean
    row_var = jnp.mean(centred * centred, axis=-1, keepdims=True)
    inverse = lax.rsqrt(row_var + 1e-05)
    return centred * inverse, inverse


def norm_back(grad_out, scaled, inverse, gain_vec):
    grad_scaled = grad_out * gain_vec
    first_mean = jnp.mean(grad_scaled, axis=-1, keepdims=True)
    second_mean = jnp.mean(grad_scaled * scaled, axis=-1, keepdims=True)
    return inverse * (grad_scaled - first_mean - scaled * second_mean)


def whole(shape):
    return pl.BlockSpec(shape, lambda *_: (0,) * len(shape))


def call(kernel, grid, in_specs, out_specs, out_shape, flops, name, scratch=()):
    bytes_accessed = sum(math.prod(s.shape) * jnp.dtype(s.dtype).itemsize for s in out_shape)
    return pl.pallas_call(
        kernel,
        grid=grid,
        in_specs=in_specs,
        out_specs=out_specs,
        out_shape=out_shape,
        scratch_shapes=list(scratch),
        compiler_params=pltpu.CompilerParams(
            vmem_limit_bytes=VMEM_BYTES, dimension_semantics=("arbitrary",) * len(grid)
        ),
        cost_estimate=pl.CostEstimate(
            flops=int(flops), bytes_accessed=2 * bytes_accessed, transcendentals=0
        ),
        name=name,
    )


def shape_of(shape, dtype):
    return jax.ShapeDtypeStruct(shape, dtype)


def project_kernel(
    hid, gain, bias, w_own, w_far, qb, coeffs, norm_t, q, k, v, mem_k, mem_v, coeffs_t
):
    scaled, _ = scaled_rows(hid[...].astype(F32))
    normed_f = scaled * gain[...] + bias[...]
    normed = normed_f.astype(BF16)
    norm_t[...] = normed.T
    half = w_own.shape[2]
    for side, weight in enumerate((w_own, w_far)):
        cols = slice(side * half, (side + 1) * half)
        q[:, cols] = (dot_nn(normed, weight[0]) + qb[0:1, cols]).astype(BF16)
        k[:, cols] = dot_nn(normed, weight[1]).astype(BF16)
        v[:, cols] = (dot_nn(normed, weight[2]) + qb[1:2, cols]).astype(BF16)

    @pl.when(pl.program_id(0) == 0)
    def _():
        rows = coeffs[...]
        coeffs_t[...] = rows.T
        for side, weight in enumerate((w_own, w_far)):
            cols = slice(side * half, (side + 1) * half)
            mem_k[:, cols] = dot_nn(rows, weight[1]).astype(BF16)
            mem_v[:, cols] = dot_nn(rows, weight[2]).astype(BF16)


def project(hid, gain, bias, w_own, w_far, qb, coeffs):
    length, width = hid.shape
    basis = coeffs.shape[0]
    rows = pl.BlockSpec((BLOCK, width), lambda i: (i, 0))
    return call(
        project_kernel,
        (length // BLOCK,),
        [
            rows,
            whole(gain.shape),
            whole(bias.shape),
            whole(w_own.shape),
            whole(w_far.shape),
            whole(qb.shape),
            whole(coeffs.shape),
        ],
        [
            pl.BlockSpec((width, BLOCK), lambda i: (0, i)),
            rows,
            rows,
            rows,
            whole((basis, width)),
            whole((basis, width)),
            whole((width, basis)),
        ],
        [
            shape_of((width, length), BF16),
            shape_of((length, width), BF16),
            shape_of((length, width), BF16),
            shape_of((length, width), BF16),
            shape_of((basis, width), BF16),
            shape_of((basis, width), BF16),
            shape_of((width, basis), BF16),
        ],
        2 * length * width * width * 3,
        "project",
    )(hid, gain, bias, w_own, w_far, qb, coeffs)


def head_rows(values_t, head):
    part = values_t[head * HD : (head + 1) * HD]
    zeros = jnp.zeros_like(part)
    return jnp.concatenate([part, zeros] if head == 0 else [zeros, part], axis=0)


def pair_maps(mw, mem_k):
    maps = dot_nn(mw, mem_k)
    row = lax.broadcasted_iota(jnp.int32, maps.shape, 0)
    lane = lax.broadcasted_iota(jnp.int32, maps.shape, 1)
    return jnp.where((row // 2) == (lane // HD), maps, 0.0)


def basis_of(logits, basis_count):
    centre = jax.nn.sigmoid(logits)
    softplus = jnp.maximum(logits, 0.0) + jnp.log(1.0 + jnp.exp(-jnp.abs(logits)))
    spread = 0.05 * softplus + (8.0 / basis_count) ** 2
    rate = -0.5 / spread
    level = lax.rsqrt(2.0 * math.pi * spread) / basis_count
    return centre, rate, level


def places_of(basis_count):
    steps = lax.broadcasted_iota(jnp.int32, (basis_count, BLOCK), 0).astype(F32)
    return (steps + 0.5) / basis_count


def attend_kernel(flag, q, k, v, mem_k, mem_v, mw, mb, att_t, mix_t, mix, stat):
    length = q.shape[0]
    basis = mem_k.shape[0]
    flag_value = flag[0, 0].astype(F32)
    q_t = (q[...].astype(F32) * 0.125).astype(BF16).T
    v_t = v[...].T
    mem_v_t = mem_v[...].T
    maps = pair_maps(mw[0].astype(BF16), mem_k[...])
    logits = add_parts(dot_nn(three_parts(maps), q_t)) + mb[0][:, 0:1]
    centre, rate, level = basis_of(logits, basis)
    places = places_of(basis)
    allowed = lax.broadcasted_iota(jnp.int32, (BLOCK, BLOCK), 0) <= lax.broadcasted_iota(
        jnp.int32, (BLOCK, BLOCK), 1
    )
    stat[4:8, :] = logits[0:4]
    for head in range(2):
        rows = slice(head * HD, (head + 1) * HD)
        q_head = head_rows(q_t, head)
        v_ones = jnp.concatenate([v_t[rows], jnp.ones((16, length), BF16)], axis=0)
        for index in range(length // BLOCK):
            start, stop = index * BLOCK, (index + 1) * BLOCK
            q_block = q_head[:, start:stop]
            near = jnp.where(allowed, dot_nn(k[start:stop, :], q_block), -1e30)
            top = jnp.max(near, axis=0, keepdims=True)
            if index:
                far = dot_nn(k[:start, :], q_block)
                top = jnp.maximum(top, jnp.max(far, axis=0, keepdims=True))
            total = dot_nn(v_ones[:, start:stop], jnp.exp(near - top).astype(BF16))
            if index:
                total += dot_nn(v_ones[:, :start], jnp.exp(far - top).astype(BF16))
            denominator = total[HD : HD + 1]
            attended = total[:HD] / denominator
            att_t[rows, start:stop] = attended
            stat[head : head + 1, start:stop] = top + jnp.log(denominator)
            offset = places - centre[2 * head : 2 * head + 1, start:stop]
            mass = (
                jnp.exp(offset * offset * rate[2 * head + 1 : 2 * head + 2, start:stop])
                * level[2 * head + 1 : 2 * head + 2, start:stop]
            )
            recalled = dot_nn(mem_v_t[rows], mass.astype(BF16))
            mix_t[rows, start:stop] = (attended + flag_value * recalled).astype(BF16)
    mix[...] = mix_t[...].T


def attend(flag, q, k, v, mem_k, mem_v, mw, mb):
    length, width = q.shape
    basis = mem_k.shape[0]
    pairs = width // 128
    rows = pl.BlockSpec((length, 128), lambda p: (0, p))
    mem_rows = pl.BlockSpec((basis, 128), lambda p: (0, p))
    cols = pl.BlockSpec((128, length), lambda p: (p, 0))
    return call(
        attend_kernel,
        (pairs,),
        [
            pl.BlockSpec(memory_space=pltpu.SMEM),
            rows,
            rows,
            rows,
            mem_rows,
            mem_rows,
            pl.BlockSpec((1, 8, basis), lambda p: (p, 0, 0)),
            pl.BlockSpec((1, 8, 128), lambda p: (p, 0, 0)),
        ],
        [cols, cols, rows, pl.BlockSpec((8, length), lambda p: (p, 0))],
        [
            shape_of((width, length), F32),
            shape_of((width, length), BF16),
            shape_of((length, width), BF16),
            shape_of((pairs * 8, length), F32),
        ],
        12 * length * length * width,
        "attend",
    )(flag, q, k, v, mem_k, mem_v, mw, mb)


def attend_back_kernel(
    flag, q, k, v, mem_k, mem_v, mw, grad, att_t, stat, dq, dk, dv, dmem_k, dmem_v, dmw, sums
):
    length = q.shape[0]
    basis = mem_k.shape[0]
    flag_value = flag[0, 0].astype(F32)
    q_t = (q[...].astype(F32) * 0.125).astype(BF16).T
    k_t = k[...].T
    grad_t = grad[...].T
    lane = lax.broadcasted_iota(jnp.int32, (length, 128), 1)
    maps = pair_maps(mw[0].astype(BF16), mem_k[...])
    logits = stat[4:8, :]
    logits = jnp.concatenate([logits, jnp.zeros_like(logits)], axis=0)
    centre, rate, level = basis_of(logits, basis)
    places = places_of(basis)
    allowed = lax.broadcasted_iota(jnp.int32, (BLOCK, BLOCK), 0) <= lax.broadcasted_iota(
        jnp.int32, (BLOCK, BLOCK), 1
    )
    q_lanes = []
    dk_lanes = []
    dv_lanes = []
    dmv_lanes = []
    mass_grads = []
    for head in range(2):
        rows = slice(head * HD, (head + 1) * HD)
        mine = (lane // HD) == head
        q_head_t = head_rows(q_t, head)
        grad_head_t = head_rows(grad_t, head)
        q_head = jnp.where(mine, q[...].astype(F32), 0.0).astype(BF16)
        grad_head = jnp.where(mine, grad[...].astype(F32), 0.0).astype(BF16)
        log_total = stat[head : head + 1, :]
        inner = jnp.sum(grad_t[rows].astype(F32) * att_t[rows], axis=0, keepdims=True)
        query_parts = [None] * (length // BLOCK)
        dk_parts = []
        dv_parts = []
        for index in range(length // BLOCK):
            start, stop = index * BLOCK, (index + 1) * BLOCK
            scores = dot_nn(k[start:stop, :], q_head_t[:, start:])
            weights = jnp.exp(scores - log_total[:, start:])
            diagonal = jnp.where(allowed, weights[:, :BLOCK], 0.0)
            if stop < length:
                weights = jnp.concatenate([diagonal, weights[:, BLOCK:]], axis=1)
            else:
                weights = diagonal
            weights_grad = dot_nn(v[start:stop, :], grad_head_t[:, start:])
            scores_grad = (weights * (weights_grad - inner[:, start:])).astype(BF16)
            dv_parts.append(dot_nn(weights.astype(BF16), grad_head[start:]))
            dk_parts.append(dot_nn(scores_grad, q_head[start:]))
            query = dot_nn(k_t[rows, start:stop], scores_grad)
            for later in range(index, length // BLOCK):
                piece = query[:, (later - index) * BLOCK : (later - index + 1) * BLOCK]
                kept = query_parts[later]
                query_parts[later] = piece if kept is None else kept + piece
        q_lanes.append(jnp.concatenate(query_parts, axis=1))
        dk_lanes.append(jnp.concatenate(dk_parts, axis=0))
        dv_lanes.append(jnp.concatenate(dv_parts, axis=0))
        sum_parts = []
        mem_total = None
        for index in range(length // BLOCK):
            start, stop = index * BLOCK, (index + 1) * BLOCK
            rate_row = rate[2 * head + 1 : 2 * head + 2, start:stop]
            offset = places - centre[2 * head : 2 * head + 1, start:stop]
            mass = (
                jnp.exp(offset * offset * rate_row) * level[2 * head + 1 : 2 * head + 2, start:stop]
            )
            basis_grad = dot_nn(mem_v[...], grad_head_t[:, start:stop])
            zeroth = basis_grad * mass
            first = zeroth * offset
            second = first * offset
            sum_parts.append(
                jnp.concatenate(
                    [
                        jnp.sum(first, axis=0, keepdims=True) * (-2.0 * rate_row),
                        jnp.sum(second, axis=0, keepdims=True) * (2.0 * rate_row * rate_row)
                        + jnp.sum(zeroth, axis=0, keepdims=True) * rate_row,
                    ],
                    axis=0,
                )
            )
            piece = dot_nn(mass.astype(BF16), grad_head[start:stop])
            mem_total = piece if mem_total is None else mem_total + piece
        dmv_lanes.append(mem_total)
        mass_grads.append(jnp.concatenate(sum_parts, axis=1))
    parity = lax.broadcasted_iota(jnp.int32, logits.shape, 0) % 2
    basis_grads = jnp.concatenate(
        mass_grads + [jnp.zeros((4, length), F32)], axis=0
    )
    slope = jnp.where(parity == 0, centre * (1.0 - centre), 0.05 * centre)
    logits_grad = basis_grads * slope * flag_value
    query_total = jnp.concatenate(q_lanes, axis=0) + dot_tn_exact(maps, logits_grad)
    dq[...] = (0.125 * query_total).T.astype(BF16)
    dk[...] = (0.125 * (dk_lanes[0] + dk_lanes[1])).astype(BF16)
    dv[...] = (dv_lanes[0] + dv_lanes[1]).astype(BF16)
    dmem_v[...] = (flag_value * (dmv_lanes[0] + dmv_lanes[1])).astype(BF16)
    row = lax.broadcasted_iota(jnp.int32, maps.shape, 0)
    lanes = lax.broadcasted_iota(jnp.int32, maps.shape, 1)
    outer = jnp.where(
        (row // 2) == (lanes // HD), add_parts(dot_nn(three_parts(logits_grad), q[...])) * 0.125, 0.0
    )
    dmem_k[...] = dot_tn_exact(mw[0], outer).astype(BF16)
    dmw[0] = add_parts(dot_nt(three_parts(outer), mem_k[...]))
    ones = jnp.ones((16, length), BF16)
    sums[0, 0:8] = jnp.broadcast_to(jnp.sum(logits_grad, axis=1, keepdims=True), (8, 128))
    sums[0, 8:9] = dot_nn(ones, dq[...])[0:1]
    sums[0, 9:10] = dot_nn(ones, dv[...])[0:1]
    sums[0, 10:16] = jnp.zeros((6, 128), F32)


def attend_back(side, flag, q, k, v, mem_k, mem_v, mw, grad, att_t, stat):
    length, width = q.shape
    basis = mem_k.shape[0]
    pairs = width // 256
    base = side * pairs
    rows = pl.BlockSpec((length, 128), lambda p: (0, base + p))
    mem_rows = pl.BlockSpec((basis, 128), lambda p: (0, base + p))
    out_rows = pl.BlockSpec((length, 128), lambda p: (0, p))
    out_mem_rows = pl.BlockSpec((basis, 128), lambda p: (0, p))
    return call(
        attend_back_kernel,
        (pairs,),
        [
            pl.BlockSpec(memory_space=pltpu.SMEM),
            rows,
            rows,
            rows,
            mem_rows,
            mem_rows,
            pl.BlockSpec((1, 8, basis), lambda p: (base + p, 0, 0)),
            rows,
            pl.BlockSpec((128, length), lambda p: (base + p, 0)),
            pl.BlockSpec((8, length), lambda p: (base + p, 0)),
        ],
        [
            out_rows,
            out_rows,
            out_rows,
            out_mem_rows,
            out_mem_rows,
            pl.BlockSpec((1, 8, basis), lambda p: (p, 0, 0)),
            pl.BlockSpec((1, 16, 128), lambda p: (p, 0, 0)),
        ],
        [
            shape_of((length, width // 2), BF16),
            shape_of((length, width // 2), BF16),
            shape_of((length, width // 2), BF16),
            shape_of((basis, width // 2), BF16),
            shape_of((basis, width // 2), BF16),
            shape_of((pairs, 8, basis), F32),
            shape_of((pairs, 16, 128), F32),
        ],
        14 * length * length * width,
        "attend_back",
    )(flag, q, k, v, mem_k, mem_v, mw, grad, att_t, stat)


def residual_kernel(mix, hid, w_own, w_far, out_bias, gain, bias, middle, normed, normed_t):
    half = w_own.shape[0]
    branch = dot_nn(mix[:, :half], w_own[...]) + dot_nn(mix[:, half:], w_far[...])
    rows = hid[...].astype(F32) + (branch + out_bias[...])
    middle[...] = rows
    scaled, _ = scaled_rows(rows)
    result = (scaled * gain[...] + bias[...]).astype(BF16)
    normed[...] = result
    normed_t[...] = result.T


def residual(mix, hid, w_own, w_far, out_bias, gain, bias):
    length, width = hid.shape
    rows = pl.BlockSpec((BLOCK, width), lambda i: (i, 0))
    return call(
        residual_kernel,
        (length // BLOCK,),
        [
            rows,
            rows,
            whole(w_own.shape),
            whole(w_far.shape),
            whole(out_bias.shape),
            whole(gain.shape),
            whole(bias.shape),
        ],
        [rows, rows, pl.BlockSpec((width, BLOCK), lambda i: (0, i))],
        [
            shape_of((length, width), F32),
            shape_of((length, width), BF16),
            shape_of((width, length), BF16),
        ],
        2 * length * width * width,
        "residual",
    )(mix, hid, w_own, w_far, out_bias, gain, bias)


def branch_back_kernel(
    normed_grad, out_grad, middle, mix_t, w_own, w_far, gain, mid_grad, mix_grad, dw_own, dw_far, sums, total
):
    index = pl.program_id(0)
    scaled, inverse = scaled_rows(middle[...])
    grad_rows = normed_grad[...]
    out_rows = out_grad[...].astype(F32)
    result = out_rows + norm_back(grad_rows, scaled, inverse, gain[...])
    mid_grad[...] = result
    branch = result.astype(BF16)
    half = w_own.shape[0]
    mix_grad[:, :half] = dot_nt(branch, w_own[...]).astype(BF16)
    mix_grad[:, half:] = dot_nt(branch, w_far[...]).astype(BF16)
    fresh = dot_nn(mix_t[...], branch)
    added = jnp.concatenate(
        [
            jnp.sum(branch.astype(F32), axis=0, keepdims=True),
            jnp.sum(grad_rows * scaled, axis=0, keepdims=True),
            jnp.sum(grad_rows, axis=0, keepdims=True),
            jnp.sum(out_rows, axis=0, keepdims=True),
            jnp.zeros((4, grad_rows.shape[1]), F32),
        ],
        axis=0,
    )

    @pl.when(index == 0)
    def _():
        total[...] = fresh
        sums[...] = added

    @pl.when(index > 0)
    def _():
        total[...] += fresh
        sums[...] += added

    @pl.when(index == pl.num_programs(0) - 1)
    def _():
        dw_own[...] = total[:half].astype(BF16)
        dw_far[...] = total[half:].astype(BF16)


def branch_back(normed_grad, out_grad, middle, mix_t, w_own, w_far, gain):
    length, width = middle.shape
    rows = pl.BlockSpec((BLOCK, width), lambda i: (i, 0))
    return call(
        branch_back_kernel,
        (length // BLOCK,),
        [
            rows,
            rows,
            rows,
            pl.BlockSpec((width, BLOCK), lambda i: (0, i)),
            whole(w_own.shape),
            whole(w_far.shape),
            whole(gain.shape),
        ],
        [rows, rows, whole(w_own.shape), whole(w_far.shape), whole((8, width))],
        [
            shape_of((length, width), F32),
            shape_of((length, width), BF16),
            shape_of(w_own.shape, BF16),
            shape_of(w_far.shape, BF16),
            shape_of((8, width), F32),
        ],
        4 * length * width * width,
        "branch_back",
        scratch=[pltpu.VMEM((width, width), F32)],
    )(normed_grad, out_grad, middle, mix_t, w_own, w_far, gain)


def feed_step(normed, normed_t, out_grad, up, up_bias, down, d_up, d_up_bias, d_down):
    weight_up = up[...]
    weight_down = down[...]
    before = dot_nn(normed[...], weight_up) + up_bias[...]
    out_rows = out_grad[...]
    hidden_grad = dot_nt(out_rows, weight_down)
    root = math.sqrt(2.0 / math.pi)
    square = before * before
    angle = jnp.tanh(before * (root + (root * 0.044715) * square))
    half_sum = 0.5 + 0.5 * angle
    activated = (before * half_sum).astype(BF16)
    slope = half_sum + before * (0.5 - 0.5 * angle * angle) * (
        root + (3.0 * 0.044715 * root) * square
    )
    before_grad = (hidden_grad * slope).astype(BF16)
    d_down[...] = dot_tn(activated, out_rows).astype(BF16)
    d_up[...] = dot_nn(normed_t[...], before_grad).astype(BF16)
    d_up_bias[...] = dot_nn(jnp.ones((8, before.shape[0]), BF16), before_grad)
    return dot_nn(activated, weight_down), dot_nt(before_grad, weight_up)


def feed_kernel(carried, steps, *refs):
    normed, normed_t, out_grad, up_far, up_own, ub_far, ub_own, down_far, down_own = refs[:9]
    refs = refs[9:]
    if carried:
        out_in, grad_in = refs[:2]
        refs = refs[2:]
    out_sum, grad_sum, du_far, du_own, dub_far, dub_own, dd_far, dd_own = refs
    index = pl.program_id(0)

    @pl.when(index == 0)
    def _():
        forward, backward = feed_step(
            normed, normed_t, out_grad, up_far, ub_far, down_far, du_far, dub_far, dd_far
        )
        if carried:
            forward += out_in[...]
            backward += grad_in[...]
        out_sum[...] = forward
        grad_sum[...] = backward

    @pl.when((index > 0) & (index < steps))
    def _():
        forward, backward = feed_step(
            normed, normed_t, out_grad, up_far, ub_far, down_far, du_far, dub_far, dd_far
        )
        out_sum[...] += forward
        grad_sum[...] += backward

    @pl.when(index >= steps)
    def _():
        forward, backward = feed_step(
            normed, normed_t, out_grad, up_own, ub_own, down_own, du_own, dub_own, dd_own
        )
        out_sum[...] += forward
        grad_sum[...] += backward


def feed(part, parts, normed, normed_t, out_grad, up_far, up_own, ub_far, ub_own, down_far, down_own, carry):
    length, width = normed.shape
    hidden = up_own.shape[1] // parts
    steps = hidden // BLOCK
    base = part * steps

    def far_block(i):
        return jnp.minimum(i, steps - 1)

    def own_block(i):
        return jnp.maximum(i - steps, 0)

    def up_spec(block, first):
        return pl.BlockSpec((width, BLOCK), lambda i: (0, first + block(i)))

    def bias_spec(block, first, rows):
        return pl.BlockSpec((rows, BLOCK), lambda i: (0, first + block(i)))

    def down_spec(block, first):
        return pl.BlockSpec((BLOCK, width), lambda i: (first + block(i), 0))

    keep = whole((length, width))
    carried = carry is not None
    specs = [
        keep,
        whole((width, length)),
        keep,
        up_spec(far_block, base),
        up_spec(own_block, base),
        bias_spec(far_block, base, 1),
        bias_spec(own_block, base, 1),
        down_spec(far_block, base),
        down_spec(own_block, base),
    ] + ([keep, keep] if carried else [])
    operands = (normed, normed_t, out_grad, up_far, up_own, ub_far, ub_own, down_far, down_own)
    return call(
        functools.partial(feed_kernel, carried, steps),
        (2 * steps,),
        specs,
        [
            keep,
            keep,
            up_spec(far_block, 0),
            up_spec(own_block, 0),
            bias_spec(far_block, 0, 8),
            bias_spec(own_block, 0, 8),
            down_spec(far_block, 0),
            down_spec(own_block, 0),
        ],
        [
            shape_of((length, width), F32),
            shape_of((length, width), F32),
            shape_of((width, hidden), BF16),
            shape_of((width, hidden), BF16),
            shape_of((8, hidden), F32),
            shape_of((8, hidden), F32),
            shape_of((hidden, width), BF16),
            shape_of((hidden, width), BF16),
        ],
        24 * length * width * hidden,
        "feed",
    )(*operands, *(carry or ()))


def weights_back_kernel(norm_t, coeffs_t, dq, dk, dv, dmem_k, dmem_v, out):
    out[0] = dot_nn(norm_t[...], dq[...]).astype(BF16)
    out[1] = (dot_nn(norm_t[...], dk[...]) + dot_nn(coeffs_t[...], dmem_k[...])).astype(BF16)
    out[2] = (dot_nn(norm_t[...], dv[...]) + dot_nn(coeffs_t[...], dmem_v[...])).astype(BF16)


def weights_back(norm_t, coeffs_t, dq, dk, dv, dmem_k, dmem_v):
    width, length = norm_t.shape
    half = dq.shape[1]
    operands = (norm_t, coeffs_t, dq, dk, dv, dmem_k, dmem_v)
    return call(
        weights_back_kernel,
        (1,),
        [whole(o.shape) for o in operands],
        [whole((3, width, half))],
        [shape_of((3, width, half), BF16)],
        6 * length * width * half,
        "weights_back",
    )(*operands)[0]


def input_back_kernel(
    hid, mid_grad, gain, w_own, w_far, dq_own, dk_own, dv_own, dq_far, dk_far, dv_far,
    dmk_own, dmv_own, dmk_far, dmv_far, in_grad, coeff_grad, sums,
):
    index = pl.program_id(0)
    grad_rows = (
        dot_nt(dq_own[...], w_own[0])
        + dot_nt(dk_own[...], w_own[1])
        + dot_nt(dv_own[...], w_own[2])
        + dot_nt(dq_far[...], w_far[0])
        + dot_nt(dk_far[...], w_far[1])
        + dot_nt(dv_far[...], w_far[2])
    )
    scaled, inverse = scaled_rows(hid[...].astype(F32))
    in_grad[...] = mid_grad[...] + norm_back(grad_rows, scaled, inverse, gain[...])
    added = jnp.concatenate(
        [
            jnp.sum(grad_rows * scaled, axis=0, keepdims=True),
            jnp.sum(grad_rows, axis=0, keepdims=True),
            jnp.zeros((6, grad_rows.shape[1]), F32),
        ],
        axis=0,
    )

    @pl.when(index == 0)
    def _():
        sums[...] = added
        coeff_grad[...] = (
            dot_nt(dmk_own[...], w_own[1])
            + dot_nt(dmv_own[...], w_own[2])
            + dot_nt(dmk_far[...], w_far[1])
            + dot_nt(dmv_far[...], w_far[2])
        )

    @pl.when(index > 0)
    def _():
        sums[...] += added


def input_back(hid, mid_grad, gain, w_own, w_far, own, far):
    length, width = hid.shape
    half = w_own.shape[2]
    basis = own[3].shape[0]
    rows = pl.BlockSpec((BLOCK, width), lambda i: (i, 0))
    half_rows = pl.BlockSpec((BLOCK, half), lambda i: (i, 0))
    return call(
        input_back_kernel,
        (length // BLOCK,),
        [rows, rows, whole(gain.shape), whole(w_own.shape), whole(w_far.shape)]
        + [half_rows] * 6
        + [whole((basis, half))] * 4,
        [rows, whole((basis, width)), whole((8, width))],
        [
            shape_of((length, width), F32),
            shape_of((basis, width), F32),
            shape_of((8, width), F32),
        ],
        6 * length * width * width,
        "input_back",
    )(hid, mid_grad, gain, w_own, w_far, *own[:3], *far[:3], *own[3:5], *far[3:5])


def to_peer(values):
    return jax.tree.map(lambda v: lax.ppermute(v, "mp", [(0, 1), (1, 0)]), values)


def across(values, offset, count):
    return lax.ppermute(values, "batch", [(i, i ^ offset) for i in range(count)])


def added(left, right):
    return (left.astype(F32) + right.astype(F32)).astype(BF16)


def halved(values, bit):
    parts = values.reshape(2, values.shape[0] // 2, values.shape[1])
    return (
        lax.dynamic_index_in_dim(parts, bit, 0, keepdims=False),
        lax.dynamic_index_in_dim(parts, 1 - bit, 0, keepdims=False),
    )


def joined(mine, theirs, bit):
    low = jnp.where(bit == 0, mine, theirs)
    high = jnp.where(bit == 0, theirs, mine)
    return jnp.concatenate([low, high], axis=0)


def sum_pair(first, second, position, count):
    bits = (position & 1, (position >> 1) & 1)
    kept = [first, second]
    for step in range(2):
        halves = [halved(kept[which], bits[step ^ which]) for which in range(2)]
        kept = [
            added(halves[which][0], across(halves[which][1], 1 << (step ^ which), count))
            for which in range(2)
        ]
    group = min(4, count // 4)
    place = (position >> 2) % group
    results = []
    for values in kept:
        parts = values.reshape(group, values.shape[0] // group, values.shape[1])
        total = lax.dynamic_index_in_dim(parts, place, 0, keepdims=False).astype(F32)
        for offset in range(1, group):
            share = lax.dynamic_index_in_dim(parts, place ^ offset, 0, keepdims=False)
            total += across(share, offset << 2, count).astype(F32)
        total = total.astype(BF16)
        offset = 4 * group
        while offset < count:
            total = added(total, across(total, offset, count))
            offset *= 2
        pieces = [total] + [across(total, offset << 2, count) for offset in range(1, group)]
        level = 1
        while level < group:
            bit = (place // level) & 1
            pieces = [
                jnp.where(bit == 0, pieces[index], pieces[index ^ level]) for index in range(group)
            ]
            level *= 2
        results.append(jnp.concatenate(pieces, axis=0))
    for step in (1, 0):
        results = [
            joined(
                results[which],
                across(results[which], 1 << (step ^ which), count),
                bits[step ^ which],
            )
            for which in range(2)
        ]
    return results


def sum_small(values, count):
    near = [across(values, offset, count) for offset in (1, 2, 3)]
    values = (values + near[0]) + (near[1] + near[2])
    offset = 4
    while offset < count:
        if offset * 2 < count:
            more = [across(values, offset * times, count) for times in (1, 2, 3)]
            values = (values + more[0]) + (more[1] + more[2])
            offset *= 4
        else:
            values = values + across(values, offset, count)
            offset *= 2
    return values


def pair_rows(values):
    heads = values.shape[1]
    rows = jnp.transpose(values, (1, 0, 2)).reshape(heads // 2, 4, values.shape[2])
    return jnp.concatenate([rows, jnp.zeros_like(rows)], axis=1)


def per_device(
    count,
    hidden_in,
    memory_flags,
    memory_coeffs,
    first_gain,
    first_bias,
    query_key_value_matrix,
    qv_bias,
    memory_weight,
    memory_bias,
    output_matrix,
    out_bias,
    second_gain,
    second_bias,
    up_matrix,
    up_bias_vector,
    down_matrix,
    down_bias,
    out_grad,
):
    me = lax.axis_index("mp")
    position = lax.axis_index("batch")
    _, tokens, width = hidden_in.shape
    first = me == 0

    def sequence(values):
        mine = lax.dynamic_index_in_dim(values, me, 0, keepdims=False)
        theirs = to_peer(lax.dynamic_index_in_dim(values, 1 - me, 0, keepdims=False))
        low = jnp.where(first, mine, theirs)
        high = jnp.where(first, theirs, mine)
        return jnp.concatenate([low, high], axis=0)

    hid = sequence(hidden_in)
    w_own = jnp.transpose(query_key_value_matrix, (1, 0, 2))
    w_far = to_peer(w_own)
    coeffs = sequence(memory_coeffs)
    small_own = (qv_bias, memory_weight, memory_bias, up_bias_vector)
    small_far = to_peer(small_own)
    wo_far = to_peer(output_matrix)
    out_rows = sequence(out_grad)
    up_far = to_peer(up_matrix)
    down_far = to_peer(down_matrix)
    flag = lax.dynamic_index_in_dim(memory_flags, me, 0, keepdims=True).reshape(1, 1)

    query_bias = jnp.concatenate([small_own[0], small_far[0]], axis=1).astype(F32)
    mem_maps = jnp.concatenate([pair_rows(small_own[1]), pair_rows(small_far[1])], axis=0)
    mem_maps = mem_maps.astype(F32)
    mem_biases = jnp.concatenate(
        [pair_rows(small_own[2][:, :, None]), pair_rows(small_far[2][:, :, None])], axis=0
    ).astype(F32)
    mem_biases = jnp.broadcast_to(mem_biases, mem_biases.shape[:2] + (128,))
    ub_own = small_own[3].astype(F32)[None]
    ub_far = small_far[3].astype(F32)[None]
    gain_one, bias_one = first_gain[None], first_bias[None]
    gain_two, bias_two = second_gain[None], second_bias[None]

    norm_t, q, k, v, mem_k, mem_v, coeffs_t = project(
        hid, gain_one, bias_one, w_own, w_far, query_bias, coeffs
    )
    att_t, mix_t, mix, stat = attend(flag, q, k, v, mem_k, mem_v, mem_maps, mem_biases)
    middle, normed, normed_t = residual(
        mix, hid, output_matrix, wo_far, out_bias[None], gain_two, bias_two
    )
    parts = 2
    carry = None
    feed_sums = []
    up_bias_far, up_bias_own = [], []
    for part in range(parts):
        out_sum, grad_sum, du_far, du_own, dub_far, dub_own, dd_far, dd_own = feed(
            part,
            parts,
            normed,
            normed_t,
            out_rows,
            up_far,
            up_matrix,
            ub_far,
            ub_own,
            down_far,
            down_matrix,
            carry,
        )
        carry = (out_sum, grad_sum)
        du_peer, dd_peer = to_peer((du_far, dd_far))
        feed_sums.append(
            sum_pair(added(du_own, du_peer), added(dd_own, dd_peer), position, count)
        )
        up_bias_far.append(dub_far[0])
        up_bias_own.append(dub_own[0])
    block_rows = (middle + carry[0] + down_bias).astype(BF16)
    mid_grad, mix_grad, dwo_own, dwo_far, mid_sums = branch_back(
        carry[1], out_rows, middle, mix_t, output_matrix, wo_far, gain_two
    )
    far = attend_back(1, flag, q, k, v, mem_k, mem_v, mem_maps, mix_grad, att_t, stat)
    dqkv_far = weights_back(norm_t, coeffs_t, *far[:5])
    own = attend_back(0, flag, q, k, v, mem_k, mem_v, mem_maps, mix_grad, att_t, stat)
    dqkv_own = weights_back(norm_t, coeffs_t, *own[:5])
    dwo_peer, dqkv_peer = to_peer((dwo_far, dqkv_far))
    half = width // 2
    bucket_far = None
    dqkv = added(dqkv_own, dqkv_peer).reshape(3 * width, half)
    dwo = added(dwo_own, dwo_peer)
    dwo = jnp.concatenate([dwo[:, :half], dwo[:, half:]], axis=0)
    bucket = jnp.concatenate([dqkv, dwo], axis=0)
    split = bucket.shape[0] // 2
    low, high = sum_pair(bucket[:split], bucket[split:], position, count)
    bucket = jnp.concatenate([low, high], axis=0).astype(F32)
    query_key_value_grad = jnp.transpose(bucket[: 3 * width].reshape(3, width, half), (1, 0, 2))
    dwo = bucket[3 * width :]
    output_matrix_grad = jnp.concatenate([dwo[:half], dwo[half:]], axis=1)
    in_rows, coeff_rows, first_sums = input_back(
        hid, mid_grad, gain_one, w_own, w_far, own, far
    )

    def own_tokens(values):
        parts_of = values.reshape(2, values.shape[0] // 2, width)
        mine = lax.dynamic_index_in_dim(parts_of, me, 0, keepdims=False)
        theirs = lax.dynamic_index_in_dim(parts_of, 1 - me, 0, keepdims=False)
        theirs = to_peer(theirs.astype(BF16)).astype(values.dtype)
        low = jnp.where(first, mine, theirs)
        high = jnp.where(first, theirs, mine)
        return jnp.stack([low, high], axis=0)

    block_out = own_tokens(block_rows)
    input_grad = own_tokens(in_rows)
    coeff_grad = own_tokens(coeff_rows)

    def flat_small(group, up_bias):
        maps, sums = group[5], group[6]
        return [
            maps[:, :4].reshape(-1),
            sums[:, :4, 0].reshape(-1),
            sums[:, 8].reshape(-1),
            sums[:, 9].reshape(-1),
            jnp.concatenate(up_bias).reshape(-1),
        ]

    shared = [mid_sums[:4].reshape(-1), first_sums[:2].reshape(-1)]
    own_small = flat_small(own, up_bias_own)
    sizes = [v.shape[0] for v in own_small + shared]
    own_flat = jnp.concatenate(own_small + shared)
    far_flat = jnp.concatenate(flat_small(far, up_bias_far) + shared)
    padding = -own_flat.shape[0] % 1024
    own_flat = jnp.pad(own_flat, (0, padding)).reshape(-1, 128)
    far_flat = jnp.pad(far_flat, (0, padding)).reshape(-1, 128)
    small = sum_small(own_flat + to_peer(far_flat), count).reshape(-1)
    pieces = []
    start = 0
    for size in sizes:
        pieces.append(small[start : start + size])
        start += size
    heads = memory_weight.shape[1]
    basis = memory_weight.shape[2]
    memory_weight_grad = jnp.transpose(pieces[0].reshape(heads, 2, basis), (1, 0, 2))
    memory_bias_grad = jnp.transpose(pieces[1].reshape(heads, 2), (1, 0))
    qv_bias_grad = jnp.stack([pieces[2], pieces[3]], axis=0)
    up_bias_grad = pieces[4]
    mid_rows = pieces[5].reshape(4, width)
    first_rows = pieces[6].reshape(2, width)
    up_weight_grad = jnp.concatenate([s[0] for s in feed_sums], axis=1).astype(F32)
    down_weight_grad = jnp.concatenate([s[1] for s in feed_sums], axis=0).astype(F32)
    return (
        block_out,
        input_grad,
        coeff_grad,
        first_rows[0],
        first_rows[1],
        query_key_value_grad,
        qv_bias_grad,
        memory_weight_grad,
        memory_bias_grad,
        output_matrix_grad,
        mid_rows[0],
        mid_rows[1],
        mid_rows[2],
        up_weight_grad,
        up_bias_grad,
        down_weight_grad,
        mid_rows[3],
    )


def solution(mesh):
    tokens = P("batch", "mp", None)
    return jax.shard_map(
        functools.partial(per_device, mesh.shape["batch"]),
        mesh=mesh,
        in_specs=(
            tokens,
            P("batch"),
            tokens,
            P(),
            P(),
            P(None, None, "mp"),
            P(None, "mp"),
            P(None, "mp", None),
            P(None, "mp"),
            P("mp", None),
            P(),
            P(),
            P(),
            P(None, "mp"),
            P("mp"),
            P("mp", None),
            P(),
            tokens,
        ),
        out_specs=(
            tokens,
            tokens,
            tokens,
            P(),
            P(),
            P(None, None, "mp"),
            P(None, "mp"),
            P(None, "mp", None),
            P(None, "mp"),
            P("mp", None),
            P(),
            P(),
            P(),
            P(None, "mp"),
            P("mp"),
            P("mp", None),
            P(),
        ),
        check_vma=False,
    )
```

time: 861 us -> 447 us (0.52)
  matrix products: 290 us -> 0 us
  waiting for transfers between devices: 299 us -> 115 us
  Pallas kernels: 0 us -> 166 us
  blocking collectives: 125 us -> 0 us
  starting transfers between devices: 0.41 us -> 74.7 us
  other arithmetic: 83.4 us -> 37.8 us
  between operations: 15.9 us -> 2.16 us
    dot_general x37 -> x0, matrix products: 290 us -> none  [the longest x33 254 us: matrix_multiply(): jnp.einsum(form, left_side, right_side, preferred_element_type=jnp.float32)]
    psum x1 -> x0, waiting for transfers between devices: 236 us -> none  [per_device(): lax.psum((qkv_grad, qv_grad, memw_grad, memb_grad, outw_grad, up_output_g...]
    pallas_call x0 -> x11, Pallas kernels: none -> 166 us  [the longest x2 52.5 us: feed(): call(functools.partial(feed_kernel, carried, steps), (2 * steps,), specs,...]
    psum x2 -> x0, blocking collectives: 122 us -> none  [the longest x1 81.6 us: per_device(): lax.psum((qkv_grad, qv_grad, memw_grad, memb_grad, outw_grad, up_output_g...]
    ppermute x0 -> x87, waiting for transfers between devices: none -> 115 us  [the longest x66 115 us: across(): lax.ppermute(values, 'batch', [(i, i ^ offset) for i in range(count)])]
    ppermute x0 -> x87, starting transfers between devices: none -> 74.7 us  [the longest x66 69.5 us: across(): lax.ppermute(values, 'batch', [(i, i ^ offset) for i in range(count)])]
    reduce_sum x11 -> x0, other arithmetic: 34.9 us -> none  [the longest x2 15.1 us: attend_forward(): denominator = jnp.sum(raised, axis=-1, keepdims=True)]
    reduce_scatter x5 -> x0, waiting for transfers between devices: 31.6 us -> none  [the longest x1 15.8 us: per_device(): lax.psum_scatter(residual_piece, 'mp', scatter_dimension=1, tiled=True)]
  transfers between devices with their start and end apart: 10 -> 87, of which waited for: 7 -> 37; matrix products, arithmetic and copies ran while one was open for 23% -> 15% of each run, Pallas kernels for 0% -> 15%
where the time goes in v1:
time: 447 us; the launch traced here: 439 us
  Pallas kernels  166 us (37%)
  waiting for transfers between devices  115 us (26%)
  starting transfers between devices  74.7 us (17%)
  local copies, waits for them, and re-layouts  42.7 us (10%)
  other arithmetic  37.8 us (8%)
    ppermute x66, waiting for transfers between devices, across(): lax.ppermute(values, 'batch', [(i, i ^ offset) for i in range(count)])  115 us
    ppermute x66, starting transfers between devices, across(): lax.ppermute(values, 'batch', [(i, i ^ offset) for i in range(count)])  69.5 us
    pallas_call x2, Pallas kernels, feed(): call(functools.partial(feed_kernel, carried, steps), (2 * steps,), specs,...  52.5 us
    pallas_call x2, Pallas kernels, attend_back(): call(attend_back_kernel, (pairs,), [pl.BlockSpec(memory_space=pltpu.SMEM)...  36.4 us
    pallas_call x1, Pallas kernels, attend(): call(attend_kernel, (pairs,), [pl.BlockSpec(memory_space=pltpu.SMEM), row...  22.6 us
    pallas_call x2, Pallas kernels, weights_back(): call(weights_back_kernel, (1,), [whole(o.shape) for o in operands], [whol...  13 us
    pallas_call x1, Pallas kernels, input_back(): call(input_back_kernel, (length // BLOCK,), [rows, rows, whole(gain.shape...  12.7 us
    pallas_call x1, Pallas kernels, project(): call(project_kernel, (length // BLOCK,), [rows, whole(gain.shape), whole(...  11.5 us
  transfers between devices with their start and end apart: 87, of which 37 were waited for; matrix products, arithmetic and copies ran while one was open for 15% of the time, Pallas kernels for 15%

profile of v1, /device:TPU:0, one launch (start us, length us, event | category | flops | bytes accessed | tf_op | source)
XLA Modules:
  0.0 438.9 jit_solution(18030969247582117928)
XLA Ops:
  0.7 2.1 dynamic-slice_bitcast_fusion.2
  9.3 2.2 dynamic-slice_bitcast_fusion.1
  30.0 11.5 %project.1 = (bf16[768,1024]{1,0:T(8,128)(2,1)}, bf16[1024,768]{1,0:T(8,128)(2,1)}, bf16[1024,768]{1,0:T(8,128)(2,1)}, bf16[1024,768]{1,0:T(8,128)(2,1)}, bf16[2...) custom-call(bf16[1024,768]{1,0:T(8,128)(2,1)} %pad_maximum_fusion.1.hid, ...), custom_call_target="tpu_custom_call" | custom-call | flops 3623878656 | bytes 14942208 | tf_op jit(solution)/shard_map/project/pallas_call | solution.py:122
  42.2 22.6 %attend.1 = (f32[768,1024]{1,0:T(8,128)}, bf16[768,1024]{1,0:T(8,128)(2,1)}, bf16[1024,768]{1,0:T(8,128)(2,1)}, f32[48,1024]{1,0:T(8,128)}) custom-call(s32[1,1]{1,0:T(1,128)} %bitcast.flag, bf16[1024,768]{1,0:T(8,128)(2,1)} %get-tuple-element.69.q, bf16[1024,768]{1,0:T(8,128)(2,1)} %get-tuple-element.70.k, bf16[1024,768]{1,0:T(8,128)(2,1)} %get-tuple-element.71.v, ...), custom_call_target="tpu_custom_call" | custom-call | flops 9663676416 | bytes 12976128 | tf_op jit(solution)/shard_map/attend/pallas_call | solution.py:235
  65.6 7.0 %residual.1 = (f32[1024,768]{1,0:T(8,128)}, bf16[1024,768]{1,0:T(8,128)(2,1)}, bf16[768,1024]{1,0:T(8,128)(2,1)}) custom-call(bf16[1024,768]{1,0:T(8,128)(2,1)} %get-tuple-element.74.mix, bf16[1024,768]{1,0:T(8,128)(2,1)} %pad_maximum_fusion.1.hid, bf16[384,768]{1,0:T(8,128)(2,1)} %w_own.3, bf16[384,768]{1,0:T(8,128)(2,1)} %copy-done.13, ...), custom_call_target="tpu_custom_call" | custom-call | flops 1207959552 | bytes 12582912 | tf_op jit(solution)/shard_map/residual/pallas_call | solution.py:429
  74.1 25.3 %feed.2 = (f32[1024,768]{1,0:T(8,128)}, f32[1024,768]{1,0:T(8,128)}, bf16[768,768]{1,0:T(8,128)(2,1)}, bf16[768,768]{1,0:T(8,128)(2,1)}, f32[8,768]{1,0:T(8,128)...) custom-call(bf16[1024,768]{1,0:T(8,128)(2,1)} %get-tuple-element.76.refs_0_, ...), custom_call_target="tpu_custom_call" | custom-call | flops 14495514624 | bytes 22118400 | tf_op jit(solution)/shard_map/feed/pallas_call | solution.py:615
  99.3 27.2 %feed.3 = (f32[1024,768]{1,0:T(8,128)}, f32[1024,768]{1,0:T(8,128)}, bf16[768,768]{1,0:T(8,128)(2,1)}, bf16[768,768]{1,0:T(8,128)(2,1)}, f32[8,768]{1,0:T(8,128)...) custom-call(bf16[1024,768]{1,0:T(8,128)(2,1)} %get-tuple-element.76.refs_0_, ...), custom_call_target="tpu_custom_call" | custom-call | flops 14495514624 | bytes 22118400 | tf_op jit(solution)/shard_map/feed/pallas_call | solution.py:615
  126.5 10.7 %branch_back.1 = (f32[1024,768]{1,0:T(8,128)}, bf16[1024,768]{1,0:T(8,128)(2,1)}, bf16[384,768]{1,0:T(8,128)(2,1)}, bf16[384,768]{1,0:T(8,128)(2,1)}, f32[8,768]{1,0:T(8,128)}) custom-call(f32[1024,768]{1,0:T(8,128)} %get-tuple-element.81.normed_grad, bf16[1024,768]{1,0:T(8,128)(2,1)} %pad_maximum_fusion.2.refs_2_.out_grad, ...), custom_call_target="tpu_custom_call" | custom-call | flops 2415919104 | bytes 11845632 | tf_op jit(solution)/shard_map/branch_back/pallas_call | solution.py:496
  137.3 18.2 %attend_back.2 = (bf16[1024,384]{1,0:T(8,128)(2,1)}, bf16[1024,384]{1,0:T(8,128)(2,1)}, bf16[1024,384]{1,0:T(8,128)(2,1)}, bf16[256,384]{1,0:T(8,128)(2,1)}, bf1...) custom-call(s32[1,1]{1,0:T(1,128)} %bitcast.flag, bf16[1024,768]{1,0:T(8,128)(2,1)} %get-tuple-element.69.q, ...), custom_call_target="tpu_custom_call" | custom-call | flops 11274289152 | bytes 5603328 | tf_op jit(solution)/shard_map/attend_back/pallas_call | solution.py:377
  155.5 18.1 %attend_back.3 = (bf16[1024,384]{1,0:T(8,128)(2,1)}, bf16[1024,384]{1,0:T(8,128)(2,1)}, bf16[1024,384]{1,0:T(8,128)(2,1)}, bf16[256,384]{1,0:T(8,128)(2,1)}, bf1...) custom-call(s32[1,1]{1,0:T(1,128)} %bitcast.flag, bf16[1024,768]{1,0:T(8,128)(2,1)} %get-tuple-element.69.q, ...), custom_call_target="tpu_custom_call" | custom-call | flops 11274289152 | bytes 5603328 | tf_op jit(solution)/shard_map/attend_back/pallas_call | solution.py:377
  175.7 6.5 %weights_back.2 = bf16[3,768,384]{2,1,0:T(8,128)(2,1)} custom-call(bf16[768,1024]{1,0:T(8,128)(2,1)} %get-tuple-element.109.norm_t, bf16[768,256]{1,0:T(8,128)(2,1)} %get-tuple-element.110.coeffs_t, bf16[1024,384]{1,0:T(8,128)(2,1)} %get-tuple-element.87.dq_own.dq, bf16[1024,384]{1,0:T(8,128)(2,1)} %get-tuple-element.88.dk_own.dk, ...), custom_call_target="tpu_custom_call" | custom-call | flops 1811939328 | bytes 3538944 | tf_op jit(solution)/shard_map/weights_back/pallas_call | solution.py:654
  182.3 6.5 %weights_back.3 = bf16[3,768,384]{2,1,0:T(8,128)(2,1)} custom-call(bf16[768,1024]{1,0:T(8,128)(2,1)} %get-tuple-element.109.norm_t, bf16[768,256]{1,0:T(8,128)(2,1)} %get-tuple-element.110.coeffs_t, bf16[1024,384]{1,0:T(8,128)(2,1)} %get-tuple-element.90.dq_far.dq, bf16[1024,384]{1,0:T(8,128)(2,1)} %get-tuple-element.91.dk_far.dk, ...), custom_call_target="tpu_custom_call" | custom-call | flops 1811939328 | bytes 3538944 | tf_op jit(solution)/shard_map/weights_back/pallas_call | solution.py:654
  188.8 12.7 %input_back.1 = (f32[1024,768]{1,0:T(8,128)}, f32[256,768]{1,0:T(8,128)}, f32[8,768]{1,0:T(8,128)}) custom-call(bf16[1024,768]{1,0:T(8,128)(2,1)} %pad_maximum_fusion.1.hid, f32[1024,768]{1,0:T(8,128)} %get-tuple-element.83.mid_grad, f32[1,768]{1,0:T(1,128)} %broadcast_in_dim.37.gain, bf16[3,768,384]{2,1,0:T(8,128)(2,1)} %bitcast.250, ...), custom_call_target="tpu_custom_call" | custom-call | flops 3623878656 | bytes 7913472 | tf_op jit(solution)/shard_map/input_back/pallas_call | solution.py:710
  206.5 2.4 fusion.8
  208.9 3.5 add_convert_fusion.1
  213.4 3.0 collective-permute-start.15
  217.9 2.1 dynamic-slice_bitcast_fusion
  220.4 2.4 collective-permute-done.17
  224.4 2.6 collective-permute-start.19
  227.3 1.7 fusion.19
  230.2 2.6 collective-permute-done.20
  232.9 2.6 slice.142
  246.6 1.9 pad_maximum_fusion
  248.5 1.7 add_convert_fusion.3
  250.8 1.7 add_convert_fusion.2
  254.2 1.7 add_convert_fusion.5
  258.5 7.9 %collective-permute-done.66 = bf16[384,768]{1,0:T(8,128)(2,1)S(1)} collective-permute-done((bf16[384,768]{1,0:T(8,128)(2,1)S(1)}, bf16[384,768]{1,0:T(8,128)(2,1)S(1)}, u32[]{:S(2)}, u32[]{:S(2)}) %collective-permute-start.66) | collective-permute-done | bytes 589856 | tf_op jit(solution)/shard_map/ppermute | solution.py:732
  267.2 11.6 %collective-permute-done.77 = bf16[384,768]{1,0:T(8,128)(2,1)S(1)} collective-permute-done((bf16[384,768]{1,0:T(8,128)(2,1)S(1)}, bf16[384,768]{1,0:T(8,128)(2,1)S(1)}, u32[]{:S(2)}, u32[]{:S(2)}) %collective-permute-start.77) | collective-permute-done | bytes 589856 | tf_op jit(solution)/shard_map/ppermute | solution.py:732
  280.4 4.4 %collective-permute-done.55 = bf16[384,768]{1,0:T(8,128)(2,1)S(1)} collective-permute-done((bf16[384,768]{1,0:T(8,128)(2,1)S(1)}, bf16[384,768]{1,0:T(8,128)(2,1)S(1)}, u32[]{:S(2)}, u32[]{:S(2)}) %collective-permute-start.55) | collective-permute-done | bytes 589856 | tf_op jit(solution)/shard_map/ppermute | solution.py:732
  287.0 4.1 collective-permute-done.67
  291.8 5.7 %collective-permute-done.78 = bf16[192,768]{1,0:T(8,128)(2,1)S(1)} collective-permute-done((bf16[192,768]{1,0:T(8,128)(2,1)S(1)}, bf16[192,768]{1,0:T(8,128)(2,1)S(1)}, u32[]{:S(2)}, u32[]{:S(2)}) %collective-permute-start.78) | collective-permute-done | bytes 294944 | tf_op jit(solution)/shard_map/ppermute | solution.py:732
  298.8 3.5 collective-permute-start.70
  305.2 3.2 collective-permute-start.81
  308.9 3.1 collective-permute-done.80
  312.0 2.8 collective-permute-start.48
  315.6 3.2 collective-permute-done.47
  318.8 2.9 collective-permute-start.59
  323.0 3.6 collective-permute-done.58
  326.7 1.9 collective-permute-start.73
  328.6 1.7 collective-permute-start.82
  330.3 4.0 collective-permute-done.72
  335.5 2.4 collective-permute-start.49
  337.8 3.5 collective-permute-done.83
  342.8 2.2 collective-permute-start.60
  345.0 3.8 collective-permute-done.50
  349.9 4.1 collective-permute-done.61
  362.7 2.3 collective-permute-done.52
  365.6 5.7 %collective-permute-done.63 = bf16[192,768]{1,0:T(8,128)(2,1)S(1)} collective-permute-done((bf16[192,768]{1,0:T(8,128)(2,1)S(1)}, bf16[192,768]{1,0:T(8,128)(2,1)S(1)}, u32[]{:S(2)}, u32[]{:S(2)}) %collective-permute-start.63) | collective-permute-done | bytes 294944 | tf_op jit(solution)/shard_map/ppermute | solution.py:732
  371.5 6.1 %collective-permute-done.23 = bf16[384,384]{1,0:T(8,128)(2,1)S(1)} collective-permute-done((bf16[384,384]{1,0:T(8,128)(2,1)S(1)}, bf16[384,384]{1,0:T(8,128)(2,1)S(1)}, u32[]{:S(2)}, u32[]{:S(2)}) %collective-permute-start.23) | collective-permute-done | bytes 294944 | tf_op jit(solution)/shard_map/ppermute | solution.py:732
  379.0 3.2 collective-permute-start.26
  383.7 3.6 collective-permute-done.25
  387.3 2.0 collective-permute-start.37
  390.9 1.6 collective-permute-done.36
  393.5 2.0 collective-permute-start.29
  398.0 1.7 collective-permute-done.29
  399.8 2.0 collective-permute-start.40
  407.3 2.5 maximum_convert_fusion.2
  409.8 5.2 %collective-permute-done.53 = bf16[384,768]{1,0:T(8,128)(2,1)S(1)} collective-permute-done((bf16[384,768]{1,0:T(8,128)(2,1)S(1)}, bf16[384,768]{1,0:T(8,128)(2,1)S(1)}, u32[]{:S(2)}, u32[]{:S(2)}) %collective-permute-start.53) | collective-permute-done | bytes 589856 | tf_op jit(solution)/shard_map/ppermute | solution.py:732
  415.3 6.1 %collective-permute-done.64 = bf16[384,768]{1,0:T(8,128)(2,1)S(1)} collective-permute-done((bf16[384,768]{1,0:T(8,128)(2,1)S(1)}, bf16[384,768]{1,0:T(8,128)(2,1)S(1)}, u32[]{:S(2)}, u32[]{:S(2)}) %collective-permute-start.64) | collective-permute-done | bytes 589856 | tf_op jit(solution)/shard_map/ppermute | solution.py:732
  421.8 1.8 collective-permute-start.31
  425.3 2.8 maximum_convert_fusion.1
  428.1 3.6 collective-permute-done.31
  432.0 2.7 collective-permute-done.42
  435.3 2.0 slice.156
  (335 shorter events, 99.5 us)
Async XLA Ops:
  2.8 19.7 %collective-permute-start = (bf16[512,768]{1,0:T(8,128)(2,1)}, bf16[512,768]{1,0:T(8,128)(2,1)}, u32[]{:S(2)}, u32[]{:S(2)}) collective-permute-start(bf16[512,768]{1,0:T(8,128)(2,1)} %dynamic-slice_bitcast_fusion.2), channel_id=1, source_target_pairs={{0,1},{1,0},{2,3},{3,2},{4,5},{5,4},{6,7},{7,6},{8,9},{9,8},{10,11... | collective-permute-start | bytes 2359304 | tf_op jit(solution)/shard_map/ppermute | solution.py:728
  3.3 25.5 %collective-permute-start.1 = (bf16[3,768,384]{2,1,0:T(8,128)(2,1)}, bf16[3,768,384]{2,1,0:T(8,128)(2,1)S(1)}, u32[]{:S(2)}, u32[]{:S(2)}) collective-permute-start(bf16[3,768,384]{2,1,0:T(8,128)(2,1)} %bitcast.248), channel_id=1, source_target_pairs={{0,1},{1,0},{2,3},{3,2},{4,5},{5,4},{6,7},{7,6},{8,9},{9,8},{10,11... | collective-permute-start | bytes 5308424 | tf_op jit(solution)/shard_map/ppermute | solution.py:728
  3.4 15.5 %collective-permute-start.4 = (bf16[2,6,256]{2,0,1:T(2,128)(2,1)}, bf16[2,6,256]{2,0,1:T(2,128)(2,1)}, u32[]{:S(2)}, u32[]{:S(2)}) collective-permute-start(bf16[2,6,256]{2,0,1:T(2,128)(2,1)} %param.25), channel_id=1, source_target_pairs={{0,1},{1,0},{2,3},{3,2},{4,5},{5,4},{6,7},{7,6},{8,9},{9,8},{10,11... | collective-permute-start | bytes 18440 | tf_op jit(solution)/shard_map/ppermute | solution.py:728
  3.8 9.2 %collective-permute-start.5 = (bf16[2,6]{1,0:T(2,128)(2,1)S(1)}, bf16[2,6]{1,0:T(2,128)(2,1)}, u32[]{:S(2)}, u32[]{:S(2)}) collective-permute-start(bf16[2,6]{1,0:T(2,128)(2,1)S(1)} %copy-done.25), channel_id=1, source_target_pairs={{0,1},{1,0},{2,3},{3,2},{4,5},{5,4},{6,7},{7,6},{8,9},{9,8},{10,11... | collective-permute-start | bytes 80 | tf_op jit(solution)/shard_map/ppermute | solution.py:728
  3.9 13.7 %collective-permute-start.9 = (bf16[1536]{0:T(1024)(128)(2,1)S(1)}, bf16[1536]{0:T(1024)(128)(2,1)}, u32[]{:S(2)}, u32[]{:S(2)}) collective-permute-start(bf16[1536]{0:T(1024)(128)(2,1)S(1)} %copy-done.24), channel_id=1, source_target_pairs={{0,1},{1,0},{2,3},{3,2},{4,5},{5,4},{6,7},{7,6},{8,9},{9,8},{10,11... | collective-permute-start | bytes 9224 | tf_op jit(solution)/shard_map/ppermute | solution.py:728
  17.5 8.0 %collective-permute-start.7 = (bf16[512,768]{1,0:T(8,128)(2,1)}, bf16[512,768]{1,0:T(8,128)(2,1)}, u32[]{:S(2)}, u32[]{:S(2)}) collective-permute-start(bf16[512,768]{1,0:T(8,128)(2,1)} %dynamic-slice_bitcast_fusion.1), channel_id=1, source_target_pairs={{0,1},{1,0},{2,3},{3,2},{4,5},{5,4},{6,7},{7,6},{8,9},{9,8},{10,11... | collective-permute-start | bytes 2359304 | tf_op jit(solution)/shard_map/ppermute | solution.py:728
  18.9 53.7 %collective-permute-start.10 = (bf16[1536,768]{1,0:T(8,128)(2,1)}, bf16[1536,768]{1,0:T(8,128)(2,1)}, u32[]{:S(2)}, u32[]{:S(2)}) collective-permute-start(bf16[1536,768]{1,0:T(8,128)(2,1)} %refs_8_.3), channel_id=1, source_target_pairs={{0,1},{1,0},{2,3},{3,2},{4,5},{5,4},{6,7},{7,6},{8,9},{9,8},{10,11... | collective-permute-start | bytes 7077896 | tf_op jit(solution)/shard_map/ppermute | solution.py:728
  20.7 52.0 %collective-permute-start.8 = (bf16[768,1536]{1,0:T(8,128)(2,1)}, bf16[768,1536]{1,0:T(8,128)(2,1)S(1)}, u32[]{:S(2)}, u32[]{:S(2)}) collective-permute-start(bf16[768,1536]{1,0:T(8,128)(2,1)} %refs_4_.3), channel_id=1, source_target_pairs={{0,1},{1,0},{2,3},{3,2},{4,5},{5,4},{6,7},{7,6},{8,9},{9,8},{10,11... | collective-permute-start | bytes 7077896 | tf_op jit(solution)/shard_map/ppermute | solution.py:728
  22.6 42.3 %collective-permute-start.6 = (bf16[384,768]{1,0:T(8,128)(2,1)S(1)}, bf16[384,768]{1,0:T(8,128)(2,1)S(1)}, u32[]{:S(2)}, u32[]{:S(2)}) collective-permute-start(bf16[384,768]{1,0:T(8,128)(2,1)S(1)} %copy-done.12), channel_id=1, source_target_pairs={{0,1},{1,0},{2,3},{3,2},{4,5},{5,4},{6,7},{7,6},{8,9},{9,8},{10,11... | collective-permute-start | bytes 1769480 | tf_op jit(solution)/shard_map/ppermute | solution.py:728
  175.2 73.2 %collective-permute-start.65 = (bf16[768,768]{1,0:T(8,128)(2,1)}, bf16[768,768]{1,0:T(8,128)(2,1)}, u32[]{:S(2)}, u32[]{:S(2)}) collective-permute-start(bf16[768,768]{1,0:T(8,128)(2,1)} %get-tuple-element.118), channel_id=1, source_target_pairs={{0,1},{1,0},{2,3},{3,2},{4,5},{5,4},{6,7},{7,6},{8,9},{9,8},{10,11... | collective-permute-start | bytes 3538952 | tf_op jit(solution)/shard_map/ppermute | solution.py:728
  175.3 75.5 %collective-permute-start.76 = (bf16[768,768]{1,0:T(8,128)(2,1)}, bf16[768,768]{1,0:T(8,128)(2,1)}, u32[]{:S(2)}, u32[]{:S(2)}) collective-permute-start(bf16[768,768]{1,0:T(8,128)(2,1)} %get-tuple-element.120), channel_id=1, source_target_pairs={{0,1},{1,0},{2,3},{3,2},{4,5},{5,4},{6,7},{7,6},{8,9},{9,8},{10,11... | collective-permute-start | bytes 3538952 | tf_op jit(solution)/shard_map/ppermute | solution.py:728
  206.4 6.9 %collective-permute-start.14 = (f32[80,128]{1,0:T(8,128)S(1)}, f32[80,128]{1,0:T(8,128)S(1)}, u32[]{:S(2)}, u32[]{:S(2)}) collective-permute-start(f32[80,128]{1,0:T(8,128)S(1)} %pad_bitcast_fusion), channel_id=1, source_target_pairs={{0,1},{1,0},{2,3},{3,2},{4,5},{5,4},{6,7},{7,6},{8,9},{9,8},{10,11... | collective-permute-start | bytes 122888 | tf_op jit(solution)/shard_map/ppermute | solution.py:728
  213.4 6.6 %collective-permute-start.15 = (f32[80,128]{1,0:T(8,128)S(1)}, f32[80,128]{1,0:T(8,128)S(1)}, u32[]{:S(2)}, u32[]{:S(2)}) collective-permute-start(f32[80,128]{1,0:T(8,128)S(1)} %bitcast_add_fusion), channel_id=1, source_target_pairs={{0,2},{2,0},{4,6},{6,4},{8,10},{10,8},{12,14},{14,12},{16,18},{18,... | collective-permute-start | bytes 122888 | tf_op jit(solution)/shard_map/ppermute | solution.py:732
  229.0 25.2 %collective-permute-start.43 = (bf16[768,768]{1,0:T(8,128)(2,1)}, bf16[768,768]{1,0:T(8,128)(2,1)}, u32[]{:S(2)}, u32[]{:S(2)}) collective-permute-start(bf16[768,768]{1,0:T(8,128)(2,1)} %get-tuple-element.114), channel_id=1, source_target_pairs={{0,1},{1,0},{2,3},{3,2},{4,5},{5,4},{6,7},{7,6},{8,9},{9,8},{10,11... | collective-permute-start | bytes 3538952 | tf_op jit(solution)/shard_map/ppermute | solution.py:728
  230.2 11.3 %collective-permute-start.32 = (bf16[384,768]{1,0:T(8,128)(2,1)}, bf16[384,768]{1,0:T(8,128)(2,1)}, u32[]{:S(2)}, u32[]{:S(2)}) collective-permute-start(bf16[384,768]{1,0:T(8,128)(2,1)} %get-tuple-element.112), channel_id=1, source_target_pairs={{0,1},{1,0},{2,3},{3,2},{4,5},{5,4},{6,7},{7,6},{8,9},{9,8},{10,11... | collective-permute-start | bytes 1769480 | tf_op jit(solution)/shard_map/ppermute | solution.py:728
  243.2 13.4 %collective-permute-start.54 = (bf16[768,768]{1,0:T(8,128)(2,1)S(1)}, bf16[768,768]{1,0:T(8,128)(2,1)S(1)}, u32[]{:S(2)}, u32[]{:S(2)}) collective-permute-start(bf16[768,768]{1,0:T(8,128)(2,1)S(1)} %copy-done.28), channel_id=1, source_target_pairs={{0,1},{1,0},{2,3},{3,2},{4,5},{5,4},{6,7},{7,6},{8,9},{9,8},{10,11... | collective-permute-start | bytes 3538952 | tf_op jit(solution)/shard_map/ppermute | solution.py:728
  244.0 41.6 %collective-permute-start.21 = (bf16[3,768,384]{2,1,0:T(8,128)(2,1)S(1)}, bf16[3,768,384]{2,1,0:T(8,128)(2,1)S(1)}, u32[]{:S(2)}, u32[]{:S(2)}) collective-permute-start(bf16[3,768,384]{2,1,0:T(8,128)(2,1)S(1)} %copy-done.27), channel_id=1, source_target_pairs={{0,1},{1,0},{2,3},{3,2},{4,5},{5,4},{6,7},{7,6},{8,9},{9,8},{10,11... | collective-permute-start | bytes 5308424 | tf_op jit(solution)/shard_map/ppermute | solution.py:728
  250.2 16.2 %collective-permute-start.66 = (bf16[384,768]{1,0:T(8,128)(2,1)S(1)}, bf16[384,768]{1,0:T(8,128)(2,1)S(1)}, u32[]{:S(2)}, u32[]{:S(2)}) collective-permute-start(bf16[384,768]{1,0:T(8,128)(2,1)S(1)} %dynamic-slice_bitcast_fusion.4), channel_id=1, source_target_pairs={{0,4},{2,6},{4,0},{6,2},{8,12},{10,14},{12,8},{14,10},{16,20},{18,... | collective-permute-start | bytes 1769480 | tf_op jit(solution)/shard_map/ppermute | solution.py:732
  252.6 26.2 %collective-permute-start.77 = (bf16[384,768]{1,0:T(8,128)(2,1)S(1)}, bf16[384,768]{1,0:T(8,128)(2,1)S(1)}, u32[]{:S(2)}, u32[]{:S(2)}) collective-permute-start(bf16[384,768]{1,0:T(8,128)(2,1)S(1)} %dynamic-slice_bitcast_fusion.3), channel_id=1, source_target_pairs={{0,4},{2,6},{4,0},{6,2},{8,12},{10,14},{12,8},{14,10},{16,20},{18,... | collective-permute-start | bytes 1769480 | tf_op jit(solution)/shard_map/ppermute | solution.py:732
  255.9 23.7 %collective-permute-start.44 = (bf16[384,768]{1,0:T(8,128)(2,1)S(1)}, bf16[384,768]{1,0:T(8,128)(2,1)S(1)}, u32[]{:S(2)}, u32[]{:S(2)}) collective-permute-start(bf16[384,768]{1,0:T(8,128)(2,1)S(1)} %dynamic-slice_bitcast_fusion.6), channel_id=1, source_target_pairs={{0,2},{2,0},{4,6},{6,4},{8,10},{10,8},{12,14},{14,12},{16,18},{18,... | collective-permute-start | bytes 1769480 | tf_op jit(solution)/shard_map/ppermute | solution.py:732
  256.9 27.9 %collective-permute-start.55 = (bf16[384,768]{1,0:T(8,128)(2,1)S(1)}, bf16[384,768]{1,0:T(8,128)(2,1)S(1)}, u32[]{:S(2)}, u32[]{:S(2)}) collective-permute-start(bf16[384,768]{1,0:T(8,128)(2,1)S(1)} %dynamic-slice_bitcast_fusion.5), channel_id=1, source_target_pairs={{0,2},{2,0},{4,6},{6,4},{8,10},{10,8},{12,14},{14,12},{16,18},{18,... | collective-permute-start | bytes 1769480 | tf_op jit(solution)/shard_map/ppermute | solution.py:732
  266.6 24.5 %collective-permute-start.67 = (bf16[192,768]{1,0:T(8,128)(2,1)S(1)}, bf16[192,768]{1,0:T(8,128)(2,1)S(1)}, u32[]{:S(2)}, u32[]{:S(2)}) collective-permute-start(bf16[192,768]{1,0:T(8,128)(2,1)S(1)} %dynamic-slice_bitcast_fusion.10), channel_id=1, source_target_pairs={{0,2},{2,0},{4,6},{6,4},{8,10},{10,8},{12,14},{14,12},{16,18},{18,... | collective-permute-start | bytes 884744 | tf_op jit(solution)/shard_map/ppermute | solution.py:732
  279.0 18.5 %collective-permute-start.78 = (bf16[192,768]{1,0:T(8,128)(2,1)S(1)}, bf16[192,768]{1,0:T(8,128)(2,1)S(1)}, u32[]{:S(2)}, u32[]{:S(2)}) collective-permute-start(bf16[192,768]{1,0:T(8,128)(2,1)S(1)} %dynamic-slice_bitcast_fusion.9), channel_id=1, source_target_pairs={{0,2},{2,0},{4,6},{6,4},{8,10},{10,8},{12,14},{14,12},{16,18},{18,... | collective-permute-start | bytes 884744 | tf_op jit(solution)/shard_map/ppermute | solution.py:732
  279.8 17.7 %collective-permute-start.45 = (bf16[192,768]{1,0:T(8,128)(2,1)S(1)}, bf16[192,768]{1,0:T(8,128)(2,1)S(1)}, u32[]{:S(2)}, u32[]{:S(2)}) collective-permute-start(bf16[192,768]{1,0:T(8,128)(2,1)S(1)} %dynamic-slice_bitcast_fusion.12), channel_id=1, source_target_pairs={{0,4},{2,6},{4,0},{6,2},{8,12},{10,14},{12,8},{14,10},{16,20},{18,... | collective-permute-start | bytes 884744 | tf_op jit(solution)/shard_map/ppermute | solution.py:732
  285.0 13.7 %collective-permute-start.56 = (bf16[192,768]{1,0:T(8,128)(2,1)S(1)}, bf16[192,768]{1,0:T(8,128)(2,1)S(1)}, u32[]{:S(2)}, u32[]{:S(2)}) collective-permute-start(bf16[192,768]{1,0:T(8,128)(2,1)S(1)} %dynamic-slice_bitcast_fusion.11), channel_id=1, source_target_pairs={{0,4},{2,6},{4,0},{6,2},{8,12},{10,14},{12,8},{14,10},{16,20},{18,... | collective-permute-start | bytes 884744 | tf_op jit(solution)/shard_map/ppermute | solution.py:732
  286.3 69.3 %collective-permute-start.22 = (bf16[768,384]{1,0:T(8,128)(2,1)S(1)}, bf16[768,384]{1,0:T(8,128)(2,1)S(1)}, u32[]{:S(2)}, u32[]{:S(2)}) collective-permute-start(bf16[768,384]{1,0:T(8,128)(2,1)S(1)} %dynamic-slice_bitcast_fusion.8), channel_id=1, source_target_pairs={{0,2},{2,0},{4,6},{6,4},{8,10},{10,8},{12,14},{14,12},{16,18},{18,... | collective-permute-start | bytes 1769480 | tf_op jit(solution)/shard_map/ppermute | solution.py:732
  291.1 66.5 %collective-permute-start.33 = (bf16[768,384]{1,0:T(8,128)(2,1)S(1)}, bf16[768,384]{1,0:T(8,128)(2,1)S(1)}, u32[]{:S(2)}, u32[]{:S(2)}) collective-permute-start(bf16[768,384]{1,0:T(8,128)(2,1)S(1)} %dynamic-slice_bitcast_fusion.7), channel_id=1, source_target_pairs={{0,4},{2,6},{4,0},{6,2},{8,12},{10,14},{12,8},{14,10},{16,20},{18,... | collective-permute-start | bytes 1769480 | tf_op jit(solution)/shard_map/ppermute | solution.py:732
  298.8 6.4 %collective-permute-start.70 = (bf16[48,768]{1,0:T(8,128)(2,1)S(1)}, bf16[48,768]{1,0:T(8,128)(2,1)S(1)}, u32[]{:S(2)}, u32[]{:S(2)}) collective-permute-start(bf16[48,768]{1,0:T(8,128)(2,1)S(1)} %get-tuple-element.187), channel_id=1, source_target_pairs={{0,24},{2,26},{4,28},{6,30},{8,16},{10,18},{12,20},{14,22},{16,8},... | collective-permute-start | bytes 221192 | tf_op jit(solution)/shard_map/ppermute | solution.py:732
  303.5 8.4 %collective-permute-start.80 = (bf16[48,768]{1,0:T(8,128)(2,1)S(1)}, bf16[48,768]{1,0:T(8,128)(2,1)S(1)}, u32[]{:S(2)}, u32[]{:S(2)}) collective-permute-start(bf16[48,768]{1,0:T(8,128)(2,1)S(1)} %get-tuple-element.195), channel_id=1, source_target_pairs={{0,16},{2,18},{4,20},{6,22},{8,24},{10,26},{12,28},{14,30},{16,0},... | collective-permute-start | bytes 221192 | tf_op jit(solution)/shard_map/ppermute | solution.py:732
  305.2 6.7 %collective-permute-start.81 = (bf16[48,768]{1,0:T(8,128)(2,1)S(1)}, bf16[48,768]{1,0:T(8,128)(2,1)S(1)}, u32[]{:S(2)}, u32[]{:S(2)}) collective-permute-start(bf16[48,768]{1,0:T(8,128)(2,1)S(1)} %get-tuple-element.194), channel_id=1, source_target_pairs={{0,24},{2,26},{4,28},{6,30},{8,16},{10,18},{12,20},{14,22},{16,8},... | collective-permute-start | bytes 221192 | tf_op jit(solution)/shard_map/ppermute | solution.py:732
  308.5 6.4 %collective-permute-start.46 = (bf16[48,768]{1,0:T(8,128)(2,1)S(1)}, bf16[48,768]{1,0:T(8,128)(2,1)S(1)}, u32[]{:S(2)}, u32[]{:S(2)}) collective-permute-start(bf16[48,768]{1,0:T(8,128)(2,1)S(1)} %get-tuple-element.200), channel_id=1, source_target_pairs={{0,8},{2,10},{4,12},{6,14},{8,0},{10,2},{12,4},{14,6},{16,24},{18,... | collective-permute-start | bytes 221192 | tf_op jit(solution)/shard_map/ppermute | solution.py:732
  312.0 6.9 %collective-permute-start.47 = (bf16[48,768]{1,0:T(8,128)(2,1)S(1)}, bf16[48,768]{1,0:T(8,128)(2,1)S(1)}, u32[]{:S(2)}, u32[]{:S(2)}) collective-permute-start(bf16[48,768]{1,0:T(8,128)(2,1)S(1)} %get-tuple-element.202), channel_id=1, source_target_pairs={{0,16},{2,18},{4,20},{6,22},{8,24},{10,26},{12,28},{14,30},{16,0},... | collective-permute-start | bytes 221192 | tf_op jit(solution)/shard_map/ppermute | solution.py:732
  312.0 6.9 %collective-permute-start.48 = (bf16[48,768]{1,0:T(8,128)(2,1)S(1)}, bf16[48,768]{1,0:T(8,128)(2,1)S(1)}, u32[]{:S(2)}, u32[]{:S(2)}) collective-permute-start(bf16[48,768]{1,0:T(8,128)(2,1)S(1)} %get-tuple-element.201), channel_id=1, source_target_pairs={{0,24},{2,26},{4,28},{6,30},{8,16},{10,18},{12,20},{14,22},{16,8},... | collective-permute-start | bytes 221192 | tf_op jit(solution)/shard_map/ppermute | solution.py:732
  314.8 7.0 %collective-permute-start.57 = (bf16[48,768]{1,0:T(8,128)(2,1)S(1)}, bf16[48,768]{1,0:T(8,128)(2,1)S(1)}, u32[]{:S(2)}, u32[]{:S(2)}) collective-permute-start(bf16[48,768]{1,0:T(8,128)(2,1)S(1)} %get-tuple-element.207), channel_id=1, source_target_pairs={{0,8},{2,10},{4,12},{6,14},{8,0},{10,2},{12,4},{14,6},{16,24},{18,... | collective-permute-start | bytes 221192 | tf_op jit(solution)/shard_map/ppermute | solution.py:732
  318.8 7.8 %collective-permute-start.58 = (bf16[48,768]{1,0:T(8,128)(2,1)S(1)}, bf16[48,768]{1,0:T(8,128)(2,1)S(1)}, u32[]{:S(2)}, u32[]{:S(2)}) collective-permute-start(bf16[48,768]{1,0:T(8,128)(2,1)S(1)} %get-tuple-element.209), channel_id=1, source_target_pairs={{0,16},{2,18},{4,20},{6,22},{8,24},{10,26},{12,28},{14,30},{16,0},... | collective-permute-start | bytes 221192 | tf_op jit(solution)/shard_map/ppermute | solution.py:732
  318.8 7.8 %collective-permute-start.59 = (bf16[48,768]{1,0:T(8,128)(2,1)S(1)}, bf16[48,768]{1,0:T(8,128)(2,1)S(1)}, u32[]{:S(2)}, u32[]{:S(2)}) collective-permute-start(bf16[48,768]{1,0:T(8,128)(2,1)S(1)} %get-tuple-element.208), channel_id=1, source_target_pairs={{0,24},{2,26},{4,28},{6,30},{8,16},{10,18},{12,20},{14,22},{16,8},... | collective-permute-start | bytes 221192 | tf_op jit(solution)/shard_map/ppermute | solution.py:732
  321.8 6.8 %collective-permute-start.71 = (bf16[48,768]{1,0:T(8,128)(2,1)S(1)}, bf16[48,768]{1,0:T(8,128)(2,1)S(1)}, u32[]{:S(2)}, u32[]{:S(2)}) collective-permute-start(bf16[48,768]{1,0:T(8,128)(2,1)S(1)} %fusion.25), channel_id=1, source_target_pairs={{0,8},{2,10},{4,12},{6,14},{8,0},{10,2},{12,4},{14,6},{16,24},{18,... | collective-permute-start | bytes 221192 | tf_op jit(solution)/shard_map/ppermute | solution.py:732
  326.7 7.6 %collective-permute-start.72 = (bf16[48,768]{1,0:T(8,128)(2,1)S(1)}, bf16[48,768]{1,0:T(8,128)(2,1)S(1)}, u32[]{:S(2)}, u32[]{:S(2)}) collective-permute-start(bf16[48,768]{1,0:T(8,128)(2,1)S(1)} %fusion.25), channel_id=1, source_target_pairs={{0,16},{2,18},{4,20},{6,22},{8,24},{10,26},{12,28},{14,30},{16,0},... | collective-permute-start | bytes 221192 | tf_op jit(solution)/shard_map/ppermute | solution.py:732
  326.7 7.6 %collective-permute-start.73 = (bf16[48,768]{1,0:T(8,128)(2,1)S(1)}, bf16[48,768]{1,0:T(8,128)(2,1)S(1)}, u32[]{:S(2)}, u32[]{:S(2)}) collective-permute-start(bf16[48,768]{1,0:T(8,128)(2,1)S(1)} %fusion.25), channel_id=1, source_target_pairs={{0,24},{2,26},{4,28},{6,30},{8,16},{10,18},{12,20},{14,22},{16,8},... | collective-permute-start | bytes 221192 | tf_op jit(solution)/shard_map/ppermute | solution.py:732
  328.6 6.9 %collective-permute-start.82 = (bf16[48,768]{1,0:T(8,128)(2,1)S(1)}, bf16[48,768]{1,0:T(8,128)(2,1)S(1)}, u32[]{:S(2)}, u32[]{:S(2)}) collective-permute-start(bf16[48,768]{1,0:T(8,128)(2,1)S(1)} %fusion.22), channel_id=1, source_target_pairs={{0,8},{2,10},{4,12},{6,14},{8,0},{10,2},{12,4},{14,6},{16,24},{18,... | collective-permute-start | bytes 221192 | tf_op jit(solution)/shard_map/ppermute | solution.py:732
  334.2 7.1 %collective-permute-start.83 = (bf16[48,768]{1,0:T(8,128)(2,1)S(1)}, bf16[48,768]{1,0:T(8,128)(2,1)S(1)}, u32[]{:S(2)}, u32[]{:S(2)}) collective-permute-start(bf16[48,768]{1,0:T(8,128)(2,1)S(1)} %fusion.22), channel_id=1, source_target_pairs={{0,16},{2,18},{4,20},{6,22},{8,24},{10,26},{12,28},{14,30},{16,0},... | collective-permute-start | bytes 221192 | tf_op jit(solution)/shard_map/ppermute | solution.py:732
  334.2 7.1 %collective-permute-start.84 = (bf16[48,768]{1,0:T(8,128)(2,1)S(1)}, bf16[48,768]{1,0:T(8,128)(2,1)S(1)}, u32[]{:S(2)}, u32[]{:S(2)}) collective-permute-start(bf16[48,768]{1,0:T(8,128)(2,1)S(1)} %fusion.22), channel_id=1, source_target_pairs={{0,24},{2,26},{4,28},{6,30},{8,16},{10,18},{12,20},{14,22},{16,8},... | collective-permute-start | bytes 221192 | tf_op jit(solution)/shard_map/ppermute | solution.py:732
  335.5 7.3 %collective-permute-start.49 = (bf16[48,768]{1,0:T(8,128)(2,1)S(1)}, bf16[48,768]{1,0:T(8,128)(2,1)S(1)}, u32[]{:S(2)}, u32[]{:S(2)}) collective-permute-start(bf16[48,768]{1,0:T(8,128)(2,1)S(1)} %fusion.31), channel_id=1, source_target_pairs={{0,8},{2,10},{4,12},{6,14},{8,0},{10,2},{12,4},{14,6},{16,24},{18,... | collective-permute-start | bytes 221192 | tf_op jit(solution)/shard_map/ppermute | solution.py:732
  341.3 7.4 %collective-permute-start.50 = (bf16[48,768]{1,0:T(8,128)(2,1)S(1)}, bf16[48,768]{1,0:T(8,128)(2,1)S(1)}, u32[]{:S(2)}, u32[]{:S(2)}) collective-permute-start(bf16[48,768]{1,0:T(8,128)(2,1)S(1)} %fusion.31), channel_id=1, source_target_pairs={{0,16},{2,18},{4,20},{6,22},{8,24},{10,26},{12,28},{14,30},{16,0},... | collective-permute-start | bytes 221192 | tf_op jit(solution)/shard_map/ppermute | solution.py:732
  341.3 7.4 %collective-permute-start.51 = (bf16[48,768]{1,0:T(8,128)(2,1)S(1)}, bf16[48,768]{1,0:T(8,128)(2,1)S(1)}, u32[]{:S(2)}, u32[]{:S(2)}) collective-permute-start(bf16[48,768]{1,0:T(8,128)(2,1)S(1)} %fusion.31), channel_id=1, source_target_pairs={{0,24},{2,26},{4,28},{6,30},{8,16},{10,18},{12,20},{14,22},{16,8},... | collective-permute-start | bytes 221192 | tf_op jit(solution)/shard_map/ppermute | solution.py:732
  342.8 6.5 %collective-permute-start.60 = (bf16[48,768]{1,0:T(8,128)(2,1)S(1)}, bf16[48,768]{1,0:T(8,128)(2,1)S(1)}, u32[]{:S(2)}, u32[]{:S(2)}) collective-permute-start(bf16[48,768]{1,0:T(8,128)(2,1)S(1)} %fusion.28), channel_id=1, source_target_pairs={{0,8},{2,10},{4,12},{6,14},{8,0},{10,2},{12,4},{14,6},{16,24},{18,... | collective-permute-start | bytes 221192 | tf_op jit(solution)/shard_map/ppermute | solution.py:732
  348.8 6.3 %collective-permute-start.62 = (bf16[48,768]{1,0:T(8,128)(2,1)S(1)}, bf16[48,768]{1,0:T(8,128)(2,1)S(1)}, u32[]{:S(2)}, u32[]{:S(2)}) collective-permute-start(bf16[48,768]{1,0:T(8,128)(2,1)S(1)} %fusion.28), channel_id=1, source_target_pairs={{0,24},{2,26},{4,28},{6,30},{8,16},{10,18},{12,20},{14,22},{16,8},... | collective-permute-start | bytes 221192 | tf_op jit(solution)/shard_map/ppermute | solution.py:732
  349.3 9.1 %collective-permute-start.74 = (bf16[192,768]{1,0:T(8,128)(2,1)S(1)}, bf16[192,768]{1,0:T(8,128)(2,1)S(1)}, u32[]{:S(2)}, u32[]{:S(2)}) collective-permute-start(bf16[192,768]{1,0:T(8,128)(2,1)S(1)} %pad_maximum_fusion.19), channel_id=1, source_target_pairs={{0,2},{2,0},{4,6},{6,4},{8,10},{10,8},{12,14},{14,12},{16,18},{18,... | collective-permute-start | bytes 884744 | tf_op jit(solution)/shard_map/ppermute | solution.py:732
  354.0 7.2 %collective-permute-start.85 = (bf16[192,768]{1,0:T(8,128)(2,1)S(1)}, bf16[192,768]{1,0:T(8,128)(2,1)S(1)}, u32[]{:S(2)}, u32[]{:S(2)}) collective-permute-start(bf16[192,768]{1,0:T(8,128)(2,1)S(1)} %pad_maximum_fusion.20), channel_id=1, source_target_pairs={{0,2},{2,0},{4,6},{6,4},{8,10},{10,8},{12,14},{14,12},{16,18},{18,... | collective-permute-start | bytes 884744 | tf_op jit(solution)/shard_map/ppermute | solution.py:732
  355.0 9.9 %collective-permute-start.52 = (bf16[192,768]{1,0:T(8,128)(2,1)S(1)}, bf16[192,768]{1,0:T(8,128)(2,1)S(1)}, u32[]{:S(2)}, u32[]{:S(2)}) collective-permute-start(bf16[192,768]{1,0:T(8,128)(2,1)S(1)} %pad_maximum_fusion.17), channel_id=1, source_target_pairs={{0,4},{2,6},{4,0},{6,2},{8,12},{10,14},{12,8},{14,10},{16,20},{18,... | collective-permute-start | bytes 884744 | tf_op jit(solution)/shard_map/ppermute | solution.py:732
  355.6 15.7 %collective-permute-start.63 = (bf16[192,768]{1,0:T(8,128)(2,1)S(1)}, bf16[192,768]{1,0:T(8,128)(2,1)S(1)}, u32[]{:S(2)}, u32[]{:S(2)}) collective-permute-start(bf16[192,768]{1,0:T(8,128)(2,1)S(1)} %pad_maximum_fusion.18), channel_id=1, source_target_pairs={{0,4},{2,6},{4,0},{6,2},{8,12},{10,14},{12,8},{14,10},{16,20},{18,... | collective-permute-start | bytes 884744 | tf_op jit(solution)/shard_map/ppermute | solution.py:732
  357.6 20.0 %collective-permute-start.23 = (bf16[384,384]{1,0:T(8,128)(2,1)S(1)}, bf16[384,384]{1,0:T(8,128)(2,1)S(1)}, u32[]{:S(2)}, u32[]{:S(2)}) collective-permute-start(bf16[384,384]{1,0:T(8,128)(2,1)S(1)} %dynamic-slice_bitcast_fusion.14), channel_id=1, source_target_pairs={{0,4},{2,6},{4,0},{6,2},{8,12},{10,14},{12,8},{14,10},{16,20},{18,... | collective-permute-start | bytes 884744 | tf_op jit(solution)/shard_map/ppermute | solution.py:732
  358.4 20.6 %collective-permute-start.34 = (bf16[384,384]{1,0:T(8,128)(2,1)S(1)}, bf16[384,384]{1,0:T(8,128)(2,1)S(1)}, u32[]{:S(2)}, u32[]{:S(2)}) collective-permute-start(bf16[384,384]{1,0:T(8,128)(2,1)S(1)} %dynamic-slice_bitcast_fusion.13), channel_id=1, source_target_pairs={{0,2},{2,0},{4,6},{6,4},{8,10},{10,8},{12,14},{14,12},{16,18},{18,... | collective-permute-start | bytes 884744 | tf_op jit(solution)/shard_map/ppermute | solution.py:732
  361.2 45.3 %collective-permute-start.75 = (bf16[384,768]{1,0:T(8,128)(2,1)S(1)}, bf16[384,768]{1,0:T(8,128)(2,1)S(1)}, u32[]{:S(2)}, u32[]{:S(2)}) collective-permute-start(bf16[384,768]{1,0:T(8,128)(2,1)S(1)} %pad_maximum_fusion.12), channel_id=1, source_target_pairs={{0,4},{2,6},{4,0},{6,2},{8,12},{10,14},{12,8},{14,10},{16,20},{18,... | collective-permute-start | bytes 1769480 | tf_op jit(solution)/shard_map/ppermute | solution.py:732
  365.0 42.1 %collective-permute-start.86 = (bf16[384,768]{1,0:T(8,128)(2,1)S(1)}, bf16[384,768]{1,0:T(8,128)(2,1)S(1)}, u32[]{:S(2)}, u32[]{:S(2)}) collective-permute-start(bf16[384,768]{1,0:T(8,128)(2,1)S(1)} %pad_maximum_fusion.13), channel_id=1, source_target_pairs={{0,4},{2,6},{4,0},{6,2},{8,12},{10,14},{12,8},{14,10},{16,20},{18,... | collective-permute-start | bytes 1769480 | tf_op jit(solution)/shard_map/ppermute | solution.py:732
  378.9 8.4 %collective-permute-start.25 = (bf16[96,384]{1,0:T(8,128)(2,1)S(1)}, bf16[96,384]{1,0:T(8,128)(2,1)S(1)}, u32[]{:S(2)}, u32[]{:S(2)}) collective-permute-start(bf16[96,384]{1,0:T(8,128)(2,1)S(1)} %get-tuple-element.216), channel_id=1, source_target_pairs={{0,16},{2,18},{4,20},{6,22},{8,24},{10,26},{12,28},{14,30},{16,0},... | collective-permute-start | bytes 221192 | tf_op jit(solution)/shard_map/ppermute | solution.py:732
  379.0 8.3 %collective-permute-start.26 = (bf16[96,384]{1,0:T(8,128)(2,1)S(1)}, bf16[96,384]{1,0:T(8,128)(2,1)S(1)}, u32[]{:S(2)}, u32[]{:S(2)}) collective-permute-start(bf16[96,384]{1,0:T(8,128)(2,1)S(1)} %get-tuple-element.215), channel_id=1, source_target_pairs={{0,24},{2,26},{4,28},{6,30},{8,16},{10,18},{12,20},{14,22},{16,8},... | collective-permute-start | bytes 221192 | tf_op jit(solution)/shard_map/ppermute | solution.py:732
  395.6 6.3 %collective-permute-start.38 = (bf16[96,384]{1,0:T(8,128)(2,1)S(1)}, bf16[96,384]{1,0:T(8,128)(2,1)S(1)}, u32[]{:S(2)}, u32[]{:S(2)}) collective-permute-start(bf16[96,384]{1,0:T(8,128)(2,1)S(1)} %fusion.34), channel_id=1, source_target_pairs={{0,8},{2,10},{4,12},{6,14},{8,0},{10,2},{12,4},{14,6},{16,24},{18,... | collective-permute-start | bytes 221192 | tf_op jit(solution)/shard_map/ppermute | solution.py:732
  401.9 13.2 %collective-permute-start.53 = (bf16[384,768]{1,0:T(8,128)(2,1)S(1)}, bf16[384,768]{1,0:T(8,128)(2,1)S(1)}, u32[]{:S(2)}, u32[]{:S(2)}) collective-permute-start(bf16[384,768]{1,0:T(8,128)(2,1)S(1)} %pad_maximum_fusion.10), channel_id=1, source_target_pairs={{0,2},{2,0},{4,6},{6,4},{8,10},{10,8},{12,14},{14,12},{16,18},{18,... | collective-permute-start | bytes 1769480 | tf_op jit(solution)/shard_map/ppermute | solution.py:732
  403.2 18.2 %collective-permute-start.64 = (bf16[384,768]{1,0:T(8,128)(2,1)S(1)}, bf16[384,768]{1,0:T(8,128)(2,1)S(1)}, u32[]{:S(2)}, u32[]{:S(2)}) collective-permute-start(bf16[384,768]{1,0:T(8,128)(2,1)S(1)} %pad_maximum_fusion.11), channel_id=1, source_target_pairs={{0,2},{2,0},{4,6},{6,4},{8,10},{10,8},{12,14},{14,12},{16,18},{18,... | collective-permute-start | bytes 1769480 | tf_op jit(solution)/shard_map/ppermute | solution.py:732
  405.9 15.7 %collective-permute-start.30 = (bf16[384,384]{1,0:T(8,128)(2,1)S(1)}, bf16[384,384]{1,0:T(8,128)(2,1)S(1)}, u32[]{:S(2)}, u32[]{:S(2)}) collective-permute-start(bf16[384,384]{1,0:T(8,128)(2,1)S(1)} %pad_maximum_fusion.15), channel_id=1, source_target_pairs={{0,4},{2,6},{4,0},{6,2},{8,12},{10,14},{12,8},{14,10},{16,20},{18,... | collective-permute-start | bytes 884744 | tf_op jit(solution)/shard_map/ppermute | solution.py:732
  406.5 18.0 %collective-permute-start.41 = (bf16[384,384]{1,0:T(8,128)(2,1)S(1)}, bf16[384,384]{1,0:T(8,128)(2,1)S(1)}, u32[]{:S(2)}, u32[]{:S(2)}) collective-permute-start(bf16[384,384]{1,0:T(8,128)(2,1)S(1)} %pad_maximum_fusion.16), channel_id=1, source_target_pairs={{0,2},{2,0},{4,6},{6,4},{8,10},{10,8},{12,14},{14,12},{16,18},{18,... | collective-permute-start | bytes 884744 | tf_op jit(solution)/shard_map/ppermute | solution.py:732
  421.8 9.9 %collective-permute-start.31 = (bf16[768,384]{1,0:T(8,128)(2,1)S(1)}, bf16[768,384]{1,0:T(8,128)(2,1)S(1)}, u32[]{:S(2)}, u32[]{:S(2)}) collective-permute-start(bf16[768,384]{1,0:T(8,128)(2,1)S(1)} %pad_maximum_fusion.8), channel_id=1, source_target_pairs={{0,2},{2,0},{4,6},{6,4},{8,10},{10,8},{12,14},{14,12},{16,18},{18,... | collective-permute-start | bytes 1769480 | tf_op jit(solution)/shard_map/ppermute | solution.py:732
  424.7 9.9 %collective-permute-start.42 = (bf16[768,384]{1,0:T(8,128)(2,1)S(1)}, bf16[768,384]{1,0:T(8,128)(2,1)S(1)}, u32[]{:S(2)}, u32[]{:S(2)}) collective-permute-start(bf16[768,384]{1,0:T(8,128)(2,1)S(1)} %pad_maximum_fusion.9), channel_id=1, source_target_pairs={{0,4},{2,6},{4,0},{6,2},{8,12},{10,14},{12,8},{14,10},{16,20},{18,... | collective-permute-start | bytes 1769480 | tf_op jit(solution)/shard_map/ppermute | solution.py:732
  (53 other events, 307.0 us)
